TPU v7x, 256 devices: a whole 4x4x8 slice. The times are simulated.
256 devices in a mesh: ctx: 128 (over y, z, x_hi, core), mp: 2 (over x_lo).
Axes of the slice: x: 4 (x_hi: 2, x_lo: 2; x = x_hi * 2 + x_lo), y: 4, z: 8, core: 2. Of those that a mesh axis runs over, the one named last changes fastest.
Arguments:
- queries: bfloat16 [98304, 512], P(('mp', 'ctx')), parts along dimension 0, may hold values from -27 to 27
- key_rows: bfloat16 [98304, 128], P(('mp', 'ctx')), parts along dimension 0, may hold values from -27 to 27
- value_rows: bfloat16 [98304, 128], P(('mp', 'ctx')), parts along dimension 0, may hold values from -6 to 6
- positions: int32 [49152], P('ctx'), may hold values from 0 to 49151, as said below
- latent_ids: int32 [98304, 8], P(('mp', 'ctx')), parts along dimension 0, may hold values from 0 to 511
- latent_acts: float32 [98304, 8], P(('mp', 'ctx')), parts along dimension 0, may hold values from 0.5 to 4
- latent_dirs: float32 [1024, 512], P('mp'), parts along dimension 0, may hold values from -2 to 2
Outputs:
- grad_queries: bfloat16 [98304, 512], P(('mp', 'ctx')), parts along dimension 0
- grad_keys: bfloat16 [98304, 128], P(('mp', 'ctx')), parts along dimension 0
- grad_values: bfloat16 [98304, 128], P(('mp', 'ctx')), parts along dimension 0
There are 2 independent parts, one for each index of `mp`. A program takes and returns all parts, laid end to end along the dimension named above; an argument that names none is the same for every part. Nothing has to cross between parts.
Inputs may be any that keep to these rules, and one draw needn't show every extreme that they name: `positions`: the position of token i is (i - r) mod 49152 for one offset r of the draw.
All inputs are finite; a program needn't handle non-finite values.
Results may differ from a plain program's by a relative error of at most 0.019.
Values may be sent and summed in bfloat16 or wider, within the bound.
No kernel may reach another device: no remote copies, remote signals or barrier semaphores. Data moves between devices by JAX's collectives and lax.ppermute only.
A program may use at most 128 MiB of HBM per device.

v0:
```python
import math

import jax
import jax.numpy as jnp
from jax import lax
from jax.sharding import PartitionSpec as P

WINDOW = 4096
SPAN = 11


def from_behind(value, axis, steps):
    count = lax.axis_size(axis)
    pairs = [(source, (source + steps) % count) for source in range(count)]
    return lax.ppermute(value, axis, pairs)


def seed_block(latent_ids, latent_acts, latent_dirs):
    columns = jnp.arange(latent_dirs.shape[0], dtype=jnp.int32)
    onehot = (latent_ids[:, :, None] == columns[None, None, :]).astype(jnp.float32)
    mixing = jnp.sum(latent_acts[:, :, None] * onehot, axis=1)
    return jnp.dot(
        mixing, latent_dirs, precision=lax.Precision.HIGHEST, preferred_element_type=jnp.float32
    ).astype(jnp.bfloat16)


def block_grads(query_block, seed_rows, key_window, value_window, query_pos, key_pos):
    row_count = query_block.shape[0]
    head_size = key_window.shape[1]
    head_count = query_block.shape[1] // head_size
    factor = 1.0 / math.sqrt(head_size)
    offsets = query_pos[:, None] - key_pos[None, :]
    visible = (offsets >= 0) & (offsets < WINDOW)
    query_heads = query_block.reshape(row_count, head_count, head_size).transpose(1, 0, 2)
    seed_heads = seed_rows.reshape(row_count, head_count, head_size).transpose(1, 0, 2)
    kept_rows = key_window.shape[0]

    def per_head(carry, inputs):
        query_one, seed_one = inputs
        scores = jnp.where(
            visible,
            jnp.dot(query_one, key_window.T, preferred_element_type=jnp.float32) * factor,
            -jnp.inf,
        )
        maxima = jnp.max(scores, axis=-1, keepdims=True)
        expos = jnp.exp(scores - maxima)
        totals = jnp.sum(expos, axis=-1, keepdims=True)
        probs = expos / totals
        probs_b = probs.astype(jnp.bfloat16)
        dprobs = jnp.dot(seed_one, value_window.T, preferred_element_type=jnp.float32)
        deltas = jnp.sum(probs * dprobs, axis=-1, keepdims=True)
        dscores = (probs * (dprobs - deltas) * factor).astype(jnp.bfloat16)
        grad_query = jnp.dot(dscores, key_window, preferred_element_type=jnp.float32)
        grad_key = jnp.dot(dscores.T, query_one, preferred_element_type=jnp.float32)
        grad_value = jnp.dot(probs_b.T, seed_one, preferred_element_type=jnp.float32)
        return (
            (carry[0] + grad_key, carry[1] + grad_value),
            (grad_query, maxima[:, 0], totals[:, 0], deltas[:, 0]),
        )

    start_acc = jnp.zeros((kept_rows, head_size), jnp.float32)
    (grad_keys, grad_values), (grad_queries, maxima, totals, deltas) = lax.scan(
        per_head, (start_acc, start_acc), (query_heads, seed_heads)
    )
    grad_queries = grad_queries.transpose(1, 0, 2).reshape(row_count, head_count * head_size)
    return (grad_queries, grad_keys, grad_values, maxima, totals, deltas)


def per_device(queries, key_rows, value_rows, positions, latent_ids, latent_acts, latent_dirs):
    block_rows = queries.shape[0]
    all_tokens = block_rows * lax.axis_size("ctx")
    seed_rows = seed_block(latent_ids, latent_acts, latent_dirs)
    paired = jnp.stack([key_rows, value_rows])
    earlier = []
    moving = paired
    for offset in range(SPAN):
        moving = from_behind(moving, "ctx", 1)
        earlier.append(moving)
    window_pairs = earlier[::-1] + [paired]
    key_window = jnp.concatenate([piece[0] for piece in window_pairs], axis=0)
    value_window = jnp.concatenate([piece[1] for piece in window_pairs], axis=0)
    key_pos = jnp.concatenate(
        [jnp.mod(positions - (SPAN - index) * block_rows, all_tokens) for index in range(SPAN + 1)],
        axis=0,
    )
    grad_q, window_k, window_v, maxima, totals, deltas = block_grads(
        queries, seed_rows, key_window, value_window, positions, key_pos
    )
    partials = jnp.stack([window_k, window_v])
    moving = partials[:, :block_rows]
    for offset in range(1, SPAN + 1):
        moving = from_behind(moving, "ctx", -1)
        moving = moving + partials[:, offset * block_rows : (offset + 1) * block_rows]
    grad_k = moving[0]
    grad_v = moving[1]
    return (grad_q.astype(jnp.bfloat16), grad_k.astype(jnp.bfloat16), grad_v.astype(jnp.bfloat16))


def solution(mesh):
    in_specs = (
        P(("mp", "ctx"), None),
        P(("mp", "ctx"), None),
        P(("mp", "ctx"), None),
        P("ctx"),
        P(("mp", "ctx"), None),
        P(("mp", "ctx"), None),
        P("mp", None),
    )
    out_specs = (P(("mp", "ctx"), None), P(("mp", "ctx"), None), P(("mp", "ctx"), None))
    return jax.shard_map(
        per_device, mesh=mesh, in_specs=in_specs, out_specs=out_specs, check_vma=False
    )
```

profile of v0, /device:TPU:2, one launch (start us, length us, event | category | flops | bytes accessed | tf_op | source)
XLA Modules:
  0.0 364.5 jit_solution(15917536640417543657)
XLA Ops:
  0.6 1.7 pad_maximum_fusion.1
  5.4 3.4 select_reduce_fusion
  11.1 1.9 copy.20
  13.1 2.3 collective-permute-done
  15.4 11.0 %collective-permute-done.1 = bf16[2,384,128]{2,1,0:T(8,128)(2,1)S(1)} collective-permute-done((bf16[2,384,128]{2,1,0:T(8,128)(2,1)}, bf16[2,384,128]{2,1,0:T(8,128)(2,1)S(1)}, u32[]{:S(2)}, u32[]{:S(2)}) %collective-permute-start.1) | collective-permute-done | bytes 196640 | tf_op jit(solution)/shard_map/ppermute | solution.py:15
  26.4 10.8 %collective-permute-done.2 = bf16[2,384,128]{2,1,0:T(8,128)(2,1)S(1)} collective-permute-done((bf16[2,384,128]{2,1,0:T(8,128)(2,1)S(1)}, bf16[2,384,128]{2,1,0:T(8,128)(2,1)S(1)}, u32[]{:S(2)}, u32[]{:S(2)}) %collective-permute-start.2) | collective-permute-done | bytes 196640 | tf_op jit(solution)/shard_map/ppermute | solution.py:15
  37.2 10.8 %collective-permute-done.3 = bf16[2,384,128]{2,1,0:T(8,128)(2,1)S(1)} collective-permute-done((bf16[2,384,128]{2,1,0:T(8,128)(2,1)S(1)}, bf16[2,384,128]{2,1,0:T(8,128)(2,1)S(1)}, u32[]{:S(2)}, u32[]{:S(2)}) %collective-permute-start.3) | collective-permute-done | bytes 196640 | tf_op jit(solution)/shard_map/ppermute | solution.py:15
  48.0 10.8 %collective-permute-done.4 = bf16[2,384,128]{2,1,0:T(8,128)(2,1)S(1)} collective-permute-done((bf16[2,384,128]{2,1,0:T(8,128)(2,1)S(1)}, bf16[2,384,128]{2,1,0:T(8,128)(2,1)S(1)}, u32[]{:S(2)}, u32[]{:S(2)}) %collective-permute-start.4) | collective-permute-done | bytes 196640 | tf_op jit(solution)/shard_map/ppermute | solution.py:15
  58.9 10.8 %collective-permute-done.5 = bf16[2,384,128]{2,1,0:T(8,128)(2,1)S(1)} collective-permute-done((bf16[2,384,128]{2,1,0:T(8,128)(2,1)S(1)}, bf16[2,384,128]{2,1,0:T(8,128)(2,1)S(1)}, u32[]{:S(2)}, u32[]{:S(2)}) %collective-permute-start.5) | collective-permute-done | bytes 196640 | tf_op jit(solution)/shard_map/ppermute | solution.py:15
  69.7 10.8 %collective-permute-done.6 = bf16[2,384,128]{2,1,0:T(8,128)(2,1)S(1)} collective-permute-done((bf16[2,384,128]{2,1,0:T(8,128)(2,1)S(1)}, bf16[2,384,128]{2,1,0:T(8,128)(2,1)S(1)}, u32[]{:S(2)}, u32[]{:S(2)}) %collective-permute-start.6) | collective-permute-done | bytes 196640 | tf_op jit(solution)/shard_map/ppermute | solution.py:15
  80.5 10.8 %collective-permute-done.7 = bf16[2,384,128]{2,1,0:T(8,128)(2,1)S(1)} collective-permute-done((bf16[2,384,128]{2,1,0:T(8,128)(2,1)S(1)}, bf16[2,384,128]{2,1,0:T(8,128)(2,1)S(1)}, u32[]{:S(2)}, u32[]{:S(2)}) %collective-permute-start.7) | collective-permute-done | bytes 196640 | tf_op jit(solution)/shard_map/ppermute | solution.py:15
  91.3 10.8 %collective-permute-done.8 = bf16[2,384,128]{2,1,0:T(8,128)(2,1)S(1)} collective-permute-done((bf16[2,384,128]{2,1,0:T(8,128)(2,1)S(1)}, bf16[2,384,128]{2,1,0:T(8,128)(2,1)S(1)}, u32[]{:S(2)}, u32[]{:S(2)}) %collective-permute-start.8) | collective-permute-done | bytes 196640 | tf_op jit(solution)/shard_map/ppermute | solution.py:15
  102.1 10.8 %collective-permute-done.9 = bf16[2,384,128]{2,1,0:T(8,128)(2,1)S(1)} collective-permute-done((bf16[2,384,128]{2,1,0:T(8,128)(2,1)S(1)}, bf16[2,384,128]{2,1,0:T(8,128)(2,1)S(1)}, u32[]{:S(2)}, u32[]{:S(2)}) %collective-permute-start.9) | collective-permute-done | bytes 196640 | tf_op jit(solution)/shard_map/ppermute | solution.py:15
  113.0 10.8 %collective-permute-done.10 = bf16[2,384,128]{2,1,0:T(8,128)(2,1)S(1)} collective-permute-done((bf16[2,384,128]{2,1,0:T(8,128)(2,1)S(1)}, bf16[2,384,128]{2,1,0:T(8,128)(2,1)S(1)}, u32[]{:S(2)}, u32[]{:S(2)}) %collective-permute-start.10) | collective-permute-done | bytes 196640 | tf_op jit(solution)/shard_map/ppermute | solution.py:15
  126.5 99.9 %while.15 = (s32[]{:T(128)}, f32[4608,128]{1,0:T(8,128)S(1)}, f32[4608,128]{1,0:T(8,128)}, bf16[4,384,128]{2,1,0:T(8,128)(2,1)}, bf16[4,384,128]{1,2,0:T(8,128)(...) while((s32[]{:T(128)}, f32[4608,128]{1,0:T(8,128)S(1)}, ...), condition=%wide.region_5.6_spmd.clone, body=%wide.region_1.5_spmd.clone.sunk | while | flops 2306210816 | bytes 139827952 | solution.py:62
  126.5 3.7 %fusion.96 = (f32[384]{0:T(512)S(1)}, f32[384,4608]{1,0:T(8,128)S(1)}) fusion(bf16[4608,128]{1,0:T(8,128)(2,1)} %get-tuple-element.260, bf16[4,384,128]{1,2,0:T(8,128)(2,1)} %get-tuple-element.259, s32[]{:T(128)} %get-tuple-element.243, s32[4608]{0:T(1024)S(1)} %get-tuple-element.263, s32[384]{0:T(512)S(1)} %get-tuple-element.264), kind=kOutput, calls=%fused_computation.166.clone.1 | convolution fusion | flops 465370752 | bytes 8377856 | tf_op jit(solution)/shard_map/while/body/eval_jaxpr/dot_general | solution.py:42
  130.2 2.9 copy-done.1
  134.2 6.4 %convolution_add_fusion.5 = f32[4608,128]{1,0:T(8,128)} fusion(f32[4608,128]{1,0:T(8,128)} %get-tuple-element.245, pred[]{:T(512)S(6)} %compare.3, bf16[4,384,128]{2,1,0:T(8,128)(2,1)} %get-tuple-element.261, s32[]{:T(128)} %get-tuple-element.243, f32[384,4608]{1,0:T(8,128)} %copy-done.1, f32[384]{0:T(512)S(1)} %fusion.97, ...), kind=kOutput, calls=%fused_computation.11.clone.1 | convolution fusion | flops 459472896 | bytes 11898369 | tf_op jit(solution)/shard_map/while/body/eval_jaxpr/dot_general | solution.py:55
  140.6 2.8 multiply_reduce_fusion.2
  143.4 2.7 multiply_convert_fusion.2
  146.2 3.1 convolution_add_fusion.4
  149.2 1.7 fusion.98
  151.0 3.7 %fusion.96 = (f32[384]{0:T(512)S(1)}, f32[384,4608]{1,0:T(8,128)S(1)}) fusion(bf16[4608,128]{1,0:T(8,128)(2,1)} %get-tuple-element.260, bf16[4,384,128]{1,2,0:T(8,128)(2,1)} %get-tuple-element.259, s32[]{:T(128)} %get-tuple-element.243, s32[4608]{0:T(1024)S(1)} %get-tuple-element.263, s32[384]{0:T(512)S(1)} %get-tuple-element.264), kind=kOutput, calls=%fused_computation.166.clone.1 | convolution fusion | flops 465370752 | bytes 8377856 | tf_op jit(solution)/shard_map/while/body/eval_jaxpr/dot_general | solution.py:42
  154.7 2.9 copy-done.1
  158.7 7.1 %convolution_add_fusion.5 = f32[4608,128]{1,0:T(8,128)} fusion(f32[4608,128]{1,0:T(8,128)} %get-tuple-element.245, pred[]{:T(512)S(6)} %compare.3, bf16[4,384,128]{2,1,0:T(8,128)(2,1)} %get-tuple-element.261, s32[]{:T(128)} %get-tuple-element.243, f32[384,4608]{1,0:T(8,128)} %copy-done.1, f32[384]{0:T(512)S(1)} %fusion.97, ...), kind=kOutput, calls=%fused_computation.11.clone.1 | convolution fusion | flops 459472896 | bytes 11898369 | tf_op jit(solution)/shard_map/while/body/eval_jaxpr/dot_general | solution.py:55
  165.7 2.8 multiply_reduce_fusion.2
  168.6 2.7 multiply_convert_fusion.2
  171.3 3.1 convolution_add_fusion.4
  176.1 3.7 %fusion.96 = (f32[384]{0:T(512)S(1)}, f32[384,4608]{1,0:T(8,128)S(1)}) fusion(bf16[4608,128]{1,0:T(8,128)(2,1)} %get-tuple-element.260, bf16[4,384,128]{1,2,0:T(8,128)(2,1)} %get-tuple-element.259, s32[]{:T(128)} %get-tuple-element.243, s32[4608]{0:T(1024)S(1)} %get-tuple-element.263, s32[384]{0:T(512)S(1)} %get-tuple-element.264), kind=kOutput, calls=%fused_computation.166.clone.1 | convolution fusion | flops 465370752 | bytes 8377856 | tf_op jit(solution)/shard_map/while/body/eval_jaxpr/dot_general | solution.py:42
  179.8 2.9 copy-done.1
  183.8 7.1 %convolution_add_fusion.5 = f32[4608,128]{1,0:T(8,128)} fusion(f32[4608,128]{1,0:T(8,128)} %get-tuple-element.245, pred[]{:T(512)S(6)} %compare.3, bf16[4,384,128]{2,1,0:T(8,128)(2,1)} %get-tuple-element.261, s32[]{:T(128)} %get-tuple-element.243, f32[384,4608]{1,0:T(8,128)} %copy-done.1, f32[384]{0:T(512)S(1)} %fusion.97, ...), kind=kOutput, calls=%fused_computation.11.clone.1 | convolution fusion | flops 459472896 | bytes 11898369 | tf_op jit(solution)/shard_map/while/body/eval_jaxpr/dot_general | solution.py:55
  190.9 2.8 multiply_reduce_fusion.2
  193.7 2.7 multiply_convert_fusion.2
  196.5 3.1 convolution_add_fusion.4
  199.5 1.7 fusion.98
  201.3 3.7 %fusion.96 = (f32[384]{0:T(512)S(1)}, f32[384,4608]{1,0:T(8,128)S(1)}) fusion(bf16[4608,128]{1,0:T(8,128)(2,1)} %get-tuple-element.260, bf16[4,384,128]{1,2,0:T(8,128)(2,1)} %get-tuple-element.259, s32[]{:T(128)} %get-tuple-element.243, s32[4608]{0:T(1024)S(1)} %get-tuple-element.263, s32[384]{0:T(512)S(1)} %get-tuple-element.264), kind=kOutput, calls=%fused_computation.166.clone.1 | convolution fusion | flops 465370752 | bytes 8377856 | tf_op jit(solution)/shard_map/while/body/eval_jaxpr/dot_general | solution.py:42
  205.0 2.9 copy-done.1
  209.0 7.1 %convolution_add_fusion.5 = f32[4608,128]{1,0:T(8,128)} fusion(f32[4608,128]{1,0:T(8,128)} %get-tuple-element.245, pred[]{:T(512)S(6)} %compare.3, bf16[4,384,128]{2,1,0:T(8,128)(2,1)} %get-tuple-element.261, s32[]{:T(128)} %get-tuple-element.243, f32[384,4608]{1,0:T(8,128)} %copy-done.1, f32[384]{0:T(512)S(1)} %fusion.97, ...), kind=kOutput, calls=%fused_computation.11.clone.1 | convolution fusion | flops 459472896 | bytes 11898369 | tf_op jit(solution)/shard_map/while/body/eval_jaxpr/dot_general | solution.py:55
  216.0 2.8 multiply_reduce_fusion.2
  218.8 2.7 multiply_convert_fusion.2
  221.6 3.1 convolution_add_fusion.4
  224.7 1.7 fusion.98
  227.6 5.3 %collective-permute-done.11 = f32[2,384,128]{2,1,0:T(8,128)S(1)} collective-permute-done((f32[2,384,128]{2,1,0:T(8,128)S(1)}, f32[2,384,128]{2,1,0:T(8,128)S(1)}, u32[]{:S(2)}, u32[]{:S(2)}) %collective-permute-start.11) | collective-permute-done | bytes 393248 | tf_op jit(solution)/shard_map/ppermute | solution.py:15
  233.0 7.9 %collective-permute-start.12 = (f32[2,384,128]{2,1,0:T(8,128)S(1)}, f32[2,384,128]{2,1,0:T(8,128)S(1)}, u32[]{:S(2)}, u32[]{:S(2)}) collective-permute-start(f32[2,384,128]{2,1,0:T(8,128)S(1)} %fusion.27), channel_id=1, source_target_pairs={{0,254},{2,0},{4,2},{6,4},{8,6},{10,8},{12,10},{14,12},{16,14},{18... | collective-permute-start | bytes 1179656 | tf_op jit(solution)/shard_map/ppermute | solution.py:15
  240.9 5.3 %collective-permute-done.12 = f32[2,384,128]{2,1,0:T(8,128)S(1)} collective-permute-done((f32[2,384,128]{2,1,0:T(8,128)S(1)}, f32[2,384,128]{2,1,0:T(8,128)S(1)}, u32[]{:S(2)}, u32[]{:S(2)}) %collective-permute-start.12) | collective-permute-done | bytes 393248 | tf_op jit(solution)/shard_map/ppermute | solution.py:15
  246.2 7.7 %collective-permute-start.13 = (f32[2,384,128]{2,1,0:T(8,128)S(1)}, f32[2,384,128]{2,1,0:T(8,128)S(1)}, u32[]{:S(2)}, u32[]{:S(2)}) collective-permute-start(f32[2,384,128]{2,1,0:T(8,128)S(1)} %fusion.29), channel_id=1, source_target_pairs={{0,254},{2,0},{4,2},{6,4},{8,6},{10,8},{12,10},{14,12},{16,14},{18... | collective-permute-start | bytes 1179656 | tf_op jit(solution)/shard_map/ppermute | solution.py:15
  253.9 5.3 %collective-permute-done.13 = f32[2,384,128]{2,1,0:T(8,128)S(1)} collective-permute-done((f32[2,384,128]{2,1,0:T(8,128)S(1)}, f32[2,384,128]{2,1,0:T(8,128)S(1)}, u32[]{:S(2)}, u32[]{:S(2)}) %collective-permute-start.13) | collective-permute-done | bytes 393248 | tf_op jit(solution)/shard_map/ppermute | solution.py:15
  259.3 7.7 %collective-permute-start.14 = (f32[2,384,128]{2,1,0:T(8,128)S(1)}, f32[2,384,128]{2,1,0:T(8,128)S(1)}, u32[]{:S(2)}, u32[]{:S(2)}) collective-permute-start(f32[2,384,128]{2,1,0:T(8,128)S(1)} %fusion.31), channel_id=1, source_target_pairs={{0,254},{2,0},{4,2},{6,4},{8,6},{10,8},{12,10},{14,12},{16,14},{18... | collective-permute-start | bytes 1179656 | tf_op jit(solution)/shard_map/ppermute | solution.py:15
  267.0 5.3 %collective-permute-done.14 = f32[2,384,128]{2,1,0:T(8,128)S(1)} collective-permute-done((f32[2,384,128]{2,1,0:T(8,128)S(1)}, f32[2,384,128]{2,1,0:T(8,128)S(1)}, u32[]{:S(2)}, u32[]{:S(2)}) %collective-permute-start.14) | collective-permute-done | bytes 393248 | tf_op jit(solution)/shard_map/ppermute | solution.py:15
  272.4 7.7 %collective-permute-start.15 = (f32[2,384,128]{2,1,0:T(8,128)S(1)}, f32[2,384,128]{2,1,0:T(8,128)S(1)}, u32[]{:S(2)}, u32[]{:S(2)}) collective-permute-start(f32[2,384,128]{2,1,0:T(8,128)S(1)} %fusion.33), channel_id=1, source_target_pairs={{0,254},{2,0},{4,2},{6,4},{8,6},{10,8},{12,10},{14,12},{16,14},{18... | collective-permute-start | bytes 1179656 | tf_op jit(solution)/shard_map/ppermute | solution.py:15
  280.1 5.3 %collective-permute-done.15 = f32[2,384,128]{2,1,0:T(8,128)S(1)} collective-permute-done((f32[2,384,128]{2,1,0:T(8,128)S(1)}, f32[2,384,128]{2,1,0:T(8,128)S(1)}, u32[]{:S(2)}, u32[]{:S(2)}) %collective-permute-start.15) | collective-permute-done | bytes 393248 | tf_op jit(solution)/shard_map/ppermute | solution.py:15
  285.4 7.7 %collective-permute-start.16 = (f32[2,384,128]{2,1,0:T(8,128)S(1)}, f32[2,384,128]{2,1,0:T(8,128)S(1)}, u32[]{:S(2)}, u32[]{:S(2)}) collective-permute-start(f32[2,384,128]{2,1,0:T(8,128)S(1)} %fusion.35), channel_id=1, source_target_pairs={{0,254},{2,0},{4,2},{6,4},{8,6},{10,8},{12,10},{14,12},{16,14},{18... | collective-permute-start | bytes 1179656 | tf_op jit(solution)/shard_map/ppermute | solution.py:15
  293.1 5.3 %collective-permute-done.16 = f32[2,384,128]{2,1,0:T(8,128)S(1)} collective-permute-done((f32[2,384,128]{2,1,0:T(8,128)S(1)}, f32[2,384,128]{2,1,0:T(8,128)S(1)}, u32[]{:S(2)}, u32[]{:S(2)}) %collective-permute-start.16) | collective-permute-done | bytes 393248 | tf_op jit(solution)/shard_map/ppermute | solution.py:15
  298.5 7.7 %collective-permute-start.17 = (f32[2,384,128]{2,1,0:T(8,128)S(1)}, f32[2,384,128]{2,1,0:T(8,128)S(1)}, u32[]{:S(2)}, u32[]{:S(2)}) collective-permute-start(f32[2,384,128]{2,1,0:T(8,128)S(1)} %fusion.37), channel_id=1, source_target_pairs={{0,254},{2,0},{4,2},{6,4},{8,6},{10,8},{12,10},{14,12},{16,14},{18... | collective-permute-start | bytes 1179656 | tf_op jit(solution)/shard_map/ppermute | solution.py:15
  306.2 5.3 %collective-permute-done.17 = f32[2,384,128]{2,1,0:T(8,128)S(1)} collective-permute-done((f32[2,384,128]{2,1,0:T(8,128)S(1)}, f32[2,384,128]{2,1,0:T(8,128)S(1)}, u32[]{:S(2)}, u32[]{:S(2)}) %collective-permute-start.17) | collective-permute-done | bytes 393248 | tf_op jit(solution)/shard_map/ppermute | solution.py:15
  311.6 7.7 %collective-permute-start.18 = (f32[2,384,128]{2,1,0:T(8,128)S(1)}, f32[2,384,128]{2,1,0:T(8,128)S(1)}, u32[]{:S(2)}, u32[]{:S(2)}) collective-permute-start(f32[2,384,128]{2,1,0:T(8,128)S(1)} %fusion.39), channel_id=1, source_target_pairs={{0,254},{2,0},{4,2},{6,4},{8,6},{10,8},{12,10},{14,12},{16,14},{18... | collective-permute-start | bytes 1179656 | tf_op jit(solution)/shard_map/ppermute | solution.py:15
  319.3 5.3 %collective-permute-done.18 = f32[2,384,128]{2,1,0:T(8,128)S(1)} collective-permute-done((f32[2,384,128]{2,1,0:T(8,128)S(1)}, f32[2,384,128]{2,1,0:T(8,128)S(1)}, u32[]{:S(2)}, u32[]{:S(2)}) %collective-permute-start.18) | collective-permute-done | bytes 393248 | tf_op jit(solution)/shard_map/ppermute | solution.py:15
  324.6 7.7 %collective-permute-start.19 = (f32[2,384,128]{2,1,0:T(8,128)S(1)}, f32[2,384,128]{2,1,0:T(8,128)S(1)}, u32[]{:S(2)}, u32[]{:S(2)}) collective-permute-start(f32[2,384,128]{2,1,0:T(8,128)S(1)} %fusion.41), channel_id=1, source_target_pairs={{0,254},{2,0},{4,2},{6,4},{8,6},{10,8},{12,10},{14,12},{16,14},{18... | collective-permute-start | bytes 1179656 | tf_op jit(solution)/shard_map/ppermute | solution.py:15
  332.3 5.3 %collective-permute-done.19 = f32[2,384,128]{2,1,0:T(8,128)S(1)} collective-permute-done((f32[2,384,128]{2,1,0:T(8,128)S(1)}, f32[2,384,128]{2,1,0:T(8,128)S(1)}, u32[]{:S(2)}, u32[]{:S(2)}) %collective-permute-start.19) | collective-permute-done | bytes 393248 | tf_op jit(solution)/shard_map/ppermute | solution.py:15
  337.7 7.7 %collective-permute-start.20 = (f32[2,384,128]{2,1,0:T(8,128)S(1)}, f32[2,384,128]{2,1,0:T(8,128)S(1)}, u32[]{:S(2)}, u32[]{:S(2)}) collective-permute-start(f32[2,384,128]{2,1,0:T(8,128)S(1)} %fusion.43), channel_id=1, source_target_pairs={{0,254},{2,0},{4,2},{6,4},{8,6},{10,8},{12,10},{14,12},{16,14},{18... | collective-permute-start | bytes 1179656 | tf_op jit(solution)/shard_map/ppermute | solution.py:15
  345.4 5.3 %collective-permute-done.20 = f32[2,384,128]{2,1,0:T(8,128)S(1)} collective-permute-done((f32[2,384,128]{2,1,0:T(8,128)S(1)}, f32[2,384,128]{2,1,0:T(8,128)S(1)}, u32[]{:S(2)}, u32[]{:S(2)}) %collective-permute-start.20) | collective-permute-done | bytes 393248 | tf_op jit(solution)/shard_map/ppermute | solution.py:15
  350.8 7.7 %collective-permute-start.21 = (f32[2,384,128]{2,1,0:T(8,128)S(1)}, f32[2,384,128]{2,1,0:T(8,128)S(1)}, u32[]{:S(2)}, u32[]{:S(2)}) collective-permute-start(f32[2,384,128]{2,1,0:T(8,128)S(1)} %fusion.24), channel_id=1, source_target_pairs={{0,254},{2,0},{4,2},{6,4},{8,6},{10,8},{12,10},{14,12},{16,14},{18... | collective-permute-start | bytes 1179656 | tf_op jit(solution)/shard_map/ppermute | solution.py:15
  358.5 1.8 copy_bitcast_fusion
  360.2 3.5 collective-permute-done.21
  (104 shorter events, 16.9 us)
Async XLA Ops:
  0.6 8.2 %copy-start = (f32[512,512]{1,0:T(8,128)S(1)}, f32[512,512]{1,0:T(8,128)}, u32[]{:S(2)}) copy-start(f32[512,512]{1,0:T(8,128)} %param.15) | copy-start | bytes 3145732
  2.4 13.0 %collective-permute-start = (bf16[2,384,128]{2,1,0:T(8,128)(2,1)}, bf16[2,384,128]{2,1,0:T(8,128)(2,1)}, u32[]{:S(2)}, u32[]{:S(2)}) collective-permute-start(bf16[2,384,128]{2,1,0:T(8,128)(2,1)} %pad_maximum_fusion.1), channel_id=1, source_target_pairs={{0,2},{2,4},{4,6},{6,8},{8,10},{10,12},{12,14},{14,16},{16,18},{18... | collective-permute-start | bytes 589832 | tf_op jit(solution)/shard_map/ppermute | solution.py:15
  5.4 7.6 %copy-start.8 = (s32[384]{0:T(512)S(1)}, s32[384]{0:T(512)}, u32[]{:S(2)}) copy-start(s32[384]{0:T(512)} %param.12) | copy-start | bytes 4612
  13.0 112.0 %copy-start.6 = (bf16[384,128]{1,0:T(8,128)(2,1)S(1)}, bf16[384,128]{1,0:T(8,128)(2,1)}, u32[]{:S(2)}) copy-start(bf16[384,128]{1,0:T(8,128)(2,1)} %param.11) | copy-start | bytes 294916
  13.0 112.0 %copy-start.7 = (bf16[384,128]{1,0:T(8,128)(2,1)S(1)}, bf16[384,128]{1,0:T(8,128)(2,1)}, u32[]{:S(2)}) copy-start(bf16[384,128]{1,0:T(8,128)(2,1)} %param.10) | copy-start | bytes 294916
  15.4 11.0 %collective-permute-start.1 = (bf16[2,384,128]{2,1,0:T(8,128)(2,1)}, bf16[2,384,128]{2,1,0:T(8,128)(2,1)S(1)}, u32[]{:S(2)}, u32[]{:S(2)}) collective-permute-start(bf16[2,384,128]{2,1,0:T(8,128)(2,1)} %collective-permute-done), channel_id=1, source_target_pairs={{0,2},{2,4},{4,6},{6,8},{8,10},{10,12},{12,14},{14,16},{16,18},{18... | collective-permute-start | bytes 589832 | tf_op jit(solution)/shard_map/ppermute | solution.py:15
  26.4 10.8 %collective-permute-start.2 = (bf16[2,384,128]{2,1,0:T(8,128)(2,1)S(1)}, bf16[2,384,128]{2,1,0:T(8,128)(2,1)S(1)}, u32[]{:S(2)}, u32[]{:S(2)}) collective-permute-start(bf16[2,384,128]{2,1,0:T(8,128)(2,1)S(1)} %collective-permute-done.1), channel_id=1, source_target_pairs={{0,2},{2,4},{4,6},{6,8},{8,10},{10,12},{12,14},{14,16},{16,18},{18... | collective-permute-start | bytes 589832 | tf_op jit(solution)/shard_map/ppermute | solution.py:15
  37.2 10.8 %collective-permute-start.3 = (bf16[2,384,128]{2,1,0:T(8,128)(2,1)S(1)}, bf16[2,384,128]{2,1,0:T(8,128)(2,1)S(1)}, u32[]{:S(2)}, u32[]{:S(2)}) collective-permute-start(bf16[2,384,128]{2,1,0:T(8,128)(2,1)S(1)} %collective-permute-done.2), channel_id=1, source_target_pairs={{0,2},{2,4},{4,6},{6,8},{8,10},{10,12},{12,14},{14,16},{16,18},{18... | collective-permute-start | bytes 589832 | tf_op jit(solution)/shard_map/ppermute | solution.py:15
  48.0 10.8 %collective-permute-start.4 = (bf16[2,384,128]{2,1,0:T(8,128)(2,1)S(1)}, bf16[2,384,128]{2,1,0:T(8,128)(2,1)S(1)}, u32[]{:S(2)}, u32[]{:S(2)}) collective-permute-start(bf16[2,384,128]{2,1,0:T(8,128)(2,1)S(1)} %collective-permute-done.3), channel_id=1, source_target_pairs={{0,2},{2,4},{4,6},{6,8},{8,10},{10,12},{12,14},{14,16},{16,18},{18... | collective-permute-start | bytes 589832 | tf_op jit(solution)/shard_map/ppermute | solution.py:15
  58.8 10.8 %collective-permute-start.5 = (bf16[2,384,128]{2,1,0:T(8,128)(2,1)S(1)}, bf16[2,384,128]{2,1,0:T(8,128)(2,1)S(1)}, u32[]{:S(2)}, u32[]{:S(2)}) collective-permute-start(bf16[2,384,128]{2,1,0:T(8,128)(2,1)S(1)} %collective-permute-done.4), channel_id=1, source_target_pairs={{0,2},{2,4},{4,6},{6,8},{8,10},{10,12},{12,14},{14,16},{16,18},{18... | collective-permute-start | bytes 589832 | tf_op jit(solution)/shard_map/ppermute | solution.py:15
  69.7 10.8 %collective-permute-start.6 = (bf16[2,384,128]{2,1,0:T(8,128)(2,1)S(1)}, bf16[2,384,128]{2,1,0:T(8,128)(2,1)S(1)}, u32[]{:S(2)}, u32[]{:S(2)}) collective-permute-start(bf16[2,384,128]{2,1,0:T(8,128)(2,1)S(1)} %collective-permute-done.5), channel_id=1, source_target_pairs={{0,2},{2,4},{4,6},{6,8},{8,10},{10,12},{12,14},{14,16},{16,18},{18... | collective-permute-start | bytes 589832 | tf_op jit(solution)/shard_map/ppermute | solution.py:15
  80.5 10.8 %collective-permute-start.7 = (bf16[2,384,128]{2,1,0:T(8,128)(2,1)S(1)}, bf16[2,384,128]{2,1,0:T(8,128)(2,1)S(1)}, u32[]{:S(2)}, u32[]{:S(2)}) collective-permute-start(bf16[2,384,128]{2,1,0:T(8,128)(2,1)S(1)} %collective-permute-done.6), channel_id=1, source_target_pairs={{0,2},{2,4},{4,6},{6,8},{8,10},{10,12},{12,14},{14,16},{16,18},{18... | collective-permute-start | bytes 589832 | tf_op jit(solution)/shard_map/ppermute | solution.py:15
  91.3 10.8 %collective-permute-start.8 = (bf16[2,384,128]{2,1,0:T(8,128)(2,1)S(1)}, bf16[2,384,128]{2,1,0:T(8,128)(2,1)S(1)}, u32[]{:S(2)}, u32[]{:S(2)}) collective-permute-start(bf16[2,384,128]{2,1,0:T(8,128)(2,1)S(1)} %collective-permute-done.7), channel_id=1, source_target_pairs={{0,2},{2,4},{4,6},{6,8},{8,10},{10,12},{12,14},{14,16},{16,18},{18... | collective-permute-start | bytes 589832 | tf_op jit(solution)/shard_map/ppermute | solution.py:15
  102.1 10.8 %collective-permute-start.9 = (bf16[2,384,128]{2,1,0:T(8,128)(2,1)S(1)}, bf16[2,384,128]{2,1,0:T(8,128)(2,1)S(1)}, u32[]{:S(2)}, u32[]{:S(2)}) collective-permute-start(bf16[2,384,128]{2,1,0:T(8,128)(2,1)S(1)} %collective-permute-done.8), channel_id=1, source_target_pairs={{0,2},{2,4},{4,6},{6,8},{8,10},{10,12},{12,14},{14,16},{16,18},{18... | collective-permute-start | bytes 589832 | tf_op jit(solution)/shard_map/ppermute | solution.py:15
  112.9 10.8 %collective-permute-start.10 = (bf16[2,384,128]{2,1,0:T(8,128)(2,1)S(1)}, bf16[2,384,128]{2,1,0:T(8,128)(2,1)S(1)}, u32[]{:S(2)}, u32[]{:S(2)}) collective-permute-start(bf16[2,384,128]{2,1,0:T(8,128)(2,1)S(1)} %collective-permute-done.9), channel_id=1, source_target_pairs={{0,2},{2,4},{4,6},{6,8},{8,10},{10,12},{12,14},{14,16},{16,18},{18... | collective-permute-start | bytes 589832 | tf_op jit(solution)/shard_map/ppermute | solution.py:15
  125.1 1.0 copy-start.4
  125.1 1.4 copy-start.9
  130.2 2.9 copy-start.1
  134.2 6.4 %copy-start.2 = (f32[384,4608]{1,0:T(8,128)S(1)}, f32[384,4608]{1,0:T(8,128)}, u32[]{:S(2)}) copy-start(f32[384,4608]{1,0:T(8,128)} %copy-done.1) | copy-start | bytes 21233668 | tf_op jit(solution)/shard_map/while
  134.2 6.4 %copy-start.10 = (bf16[4608,128]{1,0:T(8,128)(2,1)S(1)}, bf16[4608,128]{1,0:T(8,128)(2,1)}, u32[]{:S(2)}) copy-start(bf16[4608,128]{1,0:T(8,128)(2,1)} %get-tuple-element.262) | copy-start | bytes 3538948 | tf_op jit(solution)/shard_map/while
  146.2 3.1 copy-start.5
  154.7 2.9 copy-start.1
  158.6 7.1 %copy-start.2 = (f32[384,4608]{1,0:T(8,128)S(1)}, f32[384,4608]{1,0:T(8,128)}, u32[]{:S(2)}) copy-start(f32[384,4608]{1,0:T(8,128)} %copy-done.1) | copy-start | bytes 21233668 | tf_op jit(solution)/shard_map/while
  158.7 7.1 %copy-start.10 = (bf16[4608,128]{1,0:T(8,128)(2,1)S(1)}, bf16[4608,128]{1,0:T(8,128)(2,1)}, u32[]{:S(2)}) copy-start(bf16[4608,128]{1,0:T(8,128)(2,1)} %get-tuple-element.262) | copy-start | bytes 3538948 | tf_op jit(solution)/shard_map/while
  171.3 3.1 copy-start.5
  179.8 2.9 copy-start.1
  183.8 7.1 %copy-start.2 = (f32[384,4608]{1,0:T(8,128)S(1)}, f32[384,4608]{1,0:T(8,128)}, u32[]{:S(2)}) copy-start(f32[384,4608]{1,0:T(8,128)} %copy-done.1) | copy-start | bytes 21233668 | tf_op jit(solution)/shard_map/while
  183.8 7.1 %copy-start.10 = (bf16[4608,128]{1,0:T(8,128)(2,1)S(1)}, bf16[4608,128]{1,0:T(8,128)(2,1)}, u32[]{:S(2)}) copy-start(bf16[4608,128]{1,0:T(8,128)(2,1)} %get-tuple-element.262) | copy-start | bytes 3538948 | tf_op jit(solution)/shard_map/while
  196.4 3.1 copy-start.5
  205.0 2.9 copy-start.1
  208.9 7.1 %copy-start.2 = (f32[384,4608]{1,0:T(8,128)S(1)}, f32[384,4608]{1,0:T(8,128)}, u32[]{:S(2)}) copy-start(f32[384,4608]{1,0:T(8,128)} %copy-done.1) | copy-start | bytes 21233668 | tf_op jit(solution)/shard_map/while
  208.9 7.1 %copy-start.10 = (bf16[4608,128]{1,0:T(8,128)(2,1)S(1)}, bf16[4608,128]{1,0:T(8,128)(2,1)}, u32[]{:S(2)}) copy-start(bf16[4608,128]{1,0:T(8,128)(2,1)} %get-tuple-element.262) | copy-start | bytes 3538948 | tf_op jit(solution)/shard_map/while
  221.6 3.1 copy-start.5
  226.4 6.5 %copy-start.3 = (f32[4608,128]{1,0:T(8,128)S(1)}, f32[4608,128]{1,0:T(8,128)}, u32[]{:S(2)}) copy-start(f32[4608,128]{1,0:T(8,128)} %get-tuple-element.54) | copy-start | bytes 7077892
  227.5 5.4 %collective-permute-start.11 = (f32[2,384,128]{2,1,0:T(8,128)S(1)}, f32[2,384,128]{2,1,0:T(8,128)S(1)}, u32[]{:S(2)}, u32[]{:S(2)}) collective-permute-start(f32[2,384,128]{2,1,0:T(8,128)S(1)} %fusion.25), channel_id=1, source_target_pairs={{0,254},{2,0},{4,2},{6,4},{8,6},{10,8},{12,10},{14,12},{16,14},{18... | collective-permute-start | bytes 1179656 | tf_op jit(solution)/shard_map/ppermute | solution.py:15
  233.0 13.2 %collective-permute-start.12 = (f32[2,384,128]{2,1,0:T(8,128)S(1)}, f32[2,384,128]{2,1,0:T(8,128)S(1)}, u32[]{:S(2)}, u32[]{:S(2)}) collective-permute-start(f32[2,384,128]{2,1,0:T(8,128)S(1)} %fusion.27), channel_id=1, source_target_pairs={{0,254},{2,0},{4,2},{6,4},{8,6},{10,8},{12,10},{14,12},{16,14},{18... | collective-permute-start | bytes 1179656 | tf_op jit(solution)/shard_map/ppermute | solution.py:15
  246.2 13.0 %collective-permute-start.13 = (f32[2,384,128]{2,1,0:T(8,128)S(1)}, f32[2,384,128]{2,1,0:T(8,128)S(1)}, u32[]{:S(2)}, u32[]{:S(2)}) collective-permute-start(f32[2,384,128]{2,1,0:T(8,128)S(1)} %fusion.29), channel_id=1, source_target_pairs={{0,254},{2,0},{4,2},{6,4},{8,6},{10,8},{12,10},{14,12},{16,14},{18... | collective-permute-start | bytes 1179656 | tf_op jit(solution)/shard_map/ppermute | solution.py:15
  259.3 13.0 %collective-permute-start.14 = (f32[2,384,128]{2,1,0:T(8,128)S(1)}, f32[2,384,128]{2,1,0:T(8,128)S(1)}, u32[]{:S(2)}, u32[]{:S(2)}) collective-permute-start(f32[2,384,128]{2,1,0:T(8,128)S(1)} %fusion.31), channel_id=1, source_target_pairs={{0,254},{2,0},{4,2},{6,4},{8,6},{10,8},{12,10},{14,12},{16,14},{18... | collective-permute-start | bytes 1179656 | tf_op jit(solution)/shard_map/ppermute | solution.py:15
  272.4 13.0 %collective-permute-start.15 = (f32[2,384,128]{2,1,0:T(8,128)S(1)}, f32[2,384,128]{2,1,0:T(8,128)S(1)}, u32[]{:S(2)}, u32[]{:S(2)}) collective-permute-start(f32[2,384,128]{2,1,0:T(8,128)S(1)} %fusion.33), channel_id=1, source_target_pairs={{0,254},{2,0},{4,2},{6,4},{8,6},{10,8},{12,10},{14,12},{16,14},{18... | collective-permute-start | bytes 1179656 | tf_op jit(solution)/shard_map/ppermute | solution.py:15
  285.4 13.0 %collective-permute-start.16 = (f32[2,384,128]{2,1,0:T(8,128)S(1)}, f32[2,384,128]{2,1,0:T(8,128)S(1)}, u32[]{:S(2)}, u32[]{:S(2)}) collective-permute-start(f32[2,384,128]{2,1,0:T(8,128)S(1)} %fusion.35), channel_id=1, source_target_pairs={{0,254},{2,0},{4,2},{6,4},{8,6},{10,8},{12,10},{14,12},{16,14},{18... | collective-permute-start | bytes 1179656 | tf_op jit(solution)/shard_map/ppermute | solution.py:15
  298.5 13.0 %collective-permute-start.17 = (f32[2,384,128]{2,1,0:T(8,128)S(1)}, f32[2,384,128]{2,1,0:T(8,128)S(1)}, u32[]{:S(2)}, u32[]{:S(2)}) collective-permute-start(f32[2,384,128]{2,1,0:T(8,128)S(1)} %fusion.37), channel_id=1, source_target_pairs={{0,254},{2,0},{4,2},{6,4},{8,6},{10,8},{12,10},{14,12},{16,14},{18... | collective-permute-start | bytes 1179656 | tf_op jit(solution)/shard_map/ppermute | solution.py:15
  311.6 13.0 %collective-permute-start.18 = (f32[2,384,128]{2,1,0:T(8,128)S(1)}, f32[2,384,128]{2,1,0:T(8,128)S(1)}, u32[]{:S(2)}, u32[]{:S(2)}) collective-permute-start(f32[2,384,128]{2,1,0:T(8,128)S(1)} %fusion.39), channel_id=1, source_target_pairs={{0,254},{2,0},{4,2},{6,4},{8,6},{10,8},{12,10},{14,12},{16,14},{18... | collective-permute-start | bytes 1179656 | tf_op jit(solution)/shard_map/ppermute | solution.py:15
  324.6 13.0 %collective-permute-start.19 = (f32[2,384,128]{2,1,0:T(8,128)S(1)}, f32[2,384,128]{2,1,0:T(8,128)S(1)}, u32[]{:S(2)}, u32[]{:S(2)}) collective-permute-start(f32[2,384,128]{2,1,0:T(8,128)S(1)} %fusion.41), channel_id=1, source_target_pairs={{0,254},{2,0},{4,2},{6,4},{8,6},{10,8},{12,10},{14,12},{16,14},{18... | collective-permute-start | bytes 1179656 | tf_op jit(solution)/shard_map/ppermute | solution.py:15
  337.7 13.0 %collective-permute-start.20 = (f32[2,384,128]{2,1,0:T(8,128)S(1)}, f32[2,384,128]{2,1,0:T(8,128)S(1)}, u32[]{:S(2)}, u32[]{:S(2)}) collective-permute-start(f32[2,384,128]{2,1,0:T(8,128)S(1)} %fusion.43), channel_id=1, source_target_pairs={{0,254},{2,0},{4,2},{6,4},{8,6},{10,8},{12,10},{14,12},{16,14},{18... | collective-permute-start | bytes 1179656 | tf_op jit(solution)/shard_map/ppermute | solution.py:15
  350.8 13.0 %collective-permute-start.21 = (f32[2,384,128]{2,1,0:T(8,128)S(1)}, f32[2,384,128]{2,1,0:T(8,128)S(1)}, u32[]{:S(2)}, u32[]{:S(2)}) collective-permute-start(f32[2,384,128]{2,1,0:T(8,128)S(1)} %fusion.24), channel_id=1, source_target_pairs={{0,254},{2,0},{4,2},{6,4},{8,6},{10,8},{12,10},{14,12},{16,14},{18... | collective-permute-start | bytes 1179656 | tf_op jit(solution)/shard_map/ppermute | solution.py:15
where the time goes:
time: 365 us
  waiting for transfers between devices  167 us (46%)
  starting transfers between devices  77.4 us (21%)
  matrix products  74.2 us (20%)
  local copies, waits for them, and re-layouts  22.4 us (6%)
  other arithmetic  22.4 us (6%)
    ppermute x22, waiting for transfers between devices, from_behind(): return lax.ppermute(value, axis, pairs)  167 us
    ppermute x22, starting transfers between devices, from_behind(): return lax.ppermute(value, axis, pairs)  77.4 us
    dot_general x4, matrix products, per_head(): jnp.dot(probs_b.T, seed_one, preferred_element_type=jnp.float32)  27.5 us
    dot_general x4, matrix products, per_head(): jnp.dot(query_one, key_window.T, preferred_element_type=jnp.float32)  14.8 us
    dot_general x4, matrix products, per_head(): grad_key = jnp.dot(dscores.T, query_one, preferred_element_type=jnp.float32)  12.2 us
    while x32, local copies, waits for them, and re-layouts  11.5 us
    dot_general x4, matrix products, per_head(): jnp.dot(seed_one, value_window.T, preferred_element_type=jnp.float32)  11.3 us
    convert_element_type x4, other arithmetic, per_head(): dscores = (probs * (dprobs - deltas) * factor).astype(jnp.bfloat16)  11 us
  transfers between devices with their start and end apart: 22, of which 22 were waited for; matrix products, arithmetic and copies ran while one was open for 3% of the time, Pallas kernels for 0%

commit v1 on v0

v1 whole, which is shorter than its diff:
```python
import functools
import math

import jax
import jax.numpy as jnp
from jax import lax
from jax.experimental import pallas as pl
from jax.experimental.pallas import tpu as pltpu
from jax.sharding import PartitionSpec as P

TEAM = 4
ROWS = 384
TILES = 3
TILE = 128
HEADS = 4
DIM = 128
WIDE = HEADS * TILE
WINDOW = 4096
FACTOR = 1.0 / math.sqrt(DIM)
SCALE = FACTOR * math.log2(math.e)
HIDE = -1e30
VMEM_LIMIT = 56 * 1024 * 1024

BF16 = jnp.bfloat16
F32 = jnp.float32


def permute(value, target):
    count = lax.axis_size("ctx")
    return lax.ppermute(value, "ctx", [(s, target(s) % count) for s in range(count)])


def dot(a, b):
    return jnp.dot(a, b, preferred_element_type=F32)


def seed_kernel(ids_ref, acts_ref, dirs_ref, seed_ref):
    latents = dirs_ref.shape[0]
    rows = ids_ref.shape[1]
    lane = lax.broadcasted_iota(jnp.int32, (latents, rows), 0)
    mixing = jnp.zeros((latents, rows), F32)
    for k in range(ids_ref.shape[0]):
        mixing = mixing + jnp.where(lane == ids_ref[k : k + 1, :], acts_ref[k : k + 1, :], 0.0)
    seed_ref[...] = lax.dot_general(
        mixing,
        dirs_ref[...],
        (((0,), (0,)), ((), ())),
        precision=lax.Precision.HIGHEST,
        preferred_element_type=F32,
    ).astype(BF16)


def seeds_of(latent_ids, latent_acts, latent_dirs):
    return pl.pallas_call(
        seed_kernel,
        out_shape=jax.ShapeDtypeStruct((latent_ids.shape[0], latent_dirs.shape[1]), BF16),
        compiler_params=pltpu.CompilerParams(vmem_limit_bytes=VMEM_LIMIT),
    )(latent_ids.T, latent_acts.T, latent_dirs)


HEAD_SCALARS = 8


def full_jobs():
    jobs = []
    for t in (2, 1, 0):
        for u in range(TEAM):
            for at in range(TILES):
                if (u, t) == (0, 0) or (u, t) == (3, 2) or (u, t, at) == (2, 2, 2):
                    continue
                jobs.append((u, at, t))
    return jobs


FULL = full_jobs()


def scalars_of(positions):
    member = lax.axis_index("ctx") % TEAM
    core = member % 2
    tokens = positions.shape[0] * lax.axis_size("ctx")
    first = positions[0]
    begin = jnp.where(first < tokens // 2, -first, tokens - first)
    slots = jnp.stack([0 * core, 1 + 2 * core, 0 * core + 2, 3 - 2 * core])
    wraps = (member + jnp.arange(TEAM) >= TEAM).astype(jnp.int32)
    jobs = jnp.array(FULL, jnp.int32)
    table = jnp.stack([slots[jobs[:, 0]], jobs[:, 1], jobs[:, 2] + wraps[jobs[:, 0]]], axis=1)
    head = jnp.concatenate([jnp.stack([begin, slots[1], slots[3], begin]), wraps])
    return jnp.concatenate([head, table.reshape(-1)]).astype(jnp.int32)


def masked_jobs(scal):
    jobs = [(0, at, 0, 0, (at + 1) * TILE, ("causal", at * TILE)) for at in range(TILES)]
    jobs.append((2, 2, 2 + scal[6], 0, ROWS, ("tail", 1)))
    jobs.append((scal[2], 0, 2 + scal[7], TILE, 2 * TILE, ("tail", 1)))
    jobs.append((scal[2], 1, 2 + scal[7], 2 * TILE, TILE, ("tail", 1)))
    return jobs


def mask_of(kind, keys):
    name, shift = kind
    key = lax.broadcasted_iota(jnp.int32, (keys, WIDE), 0)
    query = lax.broadcasted_iota(jnp.int32, (keys, WIDE), 1) % TILE
    if name == "causal":
        return key <= query + shift
    return key >= query + shift


def fill_keys(scal, kv_refs, kx_ref, vx_ref=None, kt_ref=None):
    lane = lax.broadcasted_iota(jnp.int32, (ROWS, DIM), 1)
    row = lax.broadcasted_iota(jnp.int32, (ROWS, DIM), 0)
    ones = jnp.where(lane < 3, 1.0, 0.0)
    for d, kv_ref in enumerate(kv_refs):
        before = row - TEAM * ROWS * d < scal[0]
        kx_ref[d, :, :DIM] = kv_ref[:ROWS]
        kx_ref[d, :, DIM:] = jnp.where((lane == 3) & before, HIDE, ones).astype(BF16)
        if vx_ref is not None:
            vx_ref[d, :, :DIM] = kv_ref[ROWS:]
            vx_ref[d, :, DIM:] = ones.astype(BF16)
        if kt_ref is not None:
            for j in range(TILES):
                kt_ref[d, :, j * TILE : (j + 1) * TILE] = kv_ref[j * TILE : (j + 1) * TILE].T


def row_flags(scal, slot, at):
    if slot == 0:
        offset = 0
    elif slot == 2:
        offset = 2 * ROWS - TEAM * ROWS * scal[6]
    else:
        is_one = scal[1] == slot
        offset = jnp.where(
            is_one, ROWS - TEAM * ROWS * scal[5], 3 * ROWS - TEAM * ROWS * scal[7]
        )
    query = lax.broadcasted_iota(jnp.int32, (1, WIDE), 1) % TILE
    return jnp.where(query + at * TILE + offset >= scal[0], 1.0, 0.0)


def stats_kernel(scal, *refs):
    q_refs, s_refs, kv_refs = refs[0:4], refs[4:8], refs[8:12]
    stat_ref, qt_ref, st_ref = refs[12:15]
    kx_ref, aug_ref, run_ref = refs[15:18]
    fill_keys(scal, kv_refs, kx_ref)
    aug_ref[...] = jnp.zeros_like(aug_ref)
    row8 = lax.broadcasted_iota(jnp.int32, (16, WIDE), 0)
    for slot in range(TEAM):
        for at in range(TILES):
            n = slot * TILES + at
            for h in range(HEADS):
                cut = (slice(at * TILE, (at + 1) * TILE), slice(h * DIM, (h + 1) * DIM))
                into = (n, slice(None), slice(h * TILE, (h + 1) * TILE))
                qt_ref[into] = q_refs[slot][cut].T
                st_ref[into] = s_refs[slot][cut].T
            aug_ref[n, :16] = jnp.where(row8 == 3, row_flags(scal, slot, at), 0.0).astype(BF16)
            run_ref[n, 0:1] = jnp.full((1, WIDE), 2 * HIDE, F32)
            run_ref[n, 1:3] = jnp.zeros((2, WIDE), F32)

    def job(slot, at, d, j0, keys, kind):
        n = slot * TILES + at
        qx = jnp.concatenate([qt_ref[n], aug_ref[n]], axis=0)
        s = dot(kx_ref[d, j0 : j0 + keys], qx)
        if kind is not None:
            s = jnp.where(mask_of(kind, keys), s, HIDE)
        if len(kv_refs) == 4:
            v = v_of(d, j0, keys)
        dp = dot(v, st_ref[n])
        old = run_ref[n, 0:1]
        new = jnp.maximum(old, jnp.max(s, axis=0, keepdims=True))
        p = jnp.exp2((s - new) * SCALE)
        fade = jnp.exp2((old - new) * SCALE)
        run_ref[n, 0:1] = new
        run_ref[n, 1:2] = run_ref[n, 1:2] * fade + jnp.sum(p, axis=0, keepdims=True)
        run_ref[n, 2:3] = run_ref[n, 2:3] * fade + jnp.sum(p * dp, axis=0, keepdims=True)

    v_ref = refs[18]
    for d in range(TEAM):
        v_ref[d] = kv_refs[d][ROWS:]

    def v_of(d, j0, keys):
        return v_ref[d, j0 : j0 + keys]

    def step(index, carry):
        base = HEAD_SCALARS + 3 * index
        job(scal[base], scal[base + 1], scal[base + 2], 0, ROWS, None)
        return carry

    lax.fori_loop(0, len(FULL), step, 0)
    for one in masked_jobs(scal):
        job(*one)
    for slot in range(TEAM):
        for at in range(TILES):
            n = slot * TILES + at
            total = run_ref[n, 1:2]
            stat_ref[slot, at : at + 1] = run_ref[n, 0:1] + jnp.log2(total) * (1.0 / SCALE)
            stat_ref[slot, 3 + at : 4 + at] = run_ref[n, 2:3] / total
        stat_ref[slot, 6:8] = jnp.zeros((2, WIDE), F32)


def stats_of(scal, q_slots, s_slots, kvs):
    smem = pl.BlockSpec(memory_space=pltpu.SMEM)
    vmem = pl.BlockSpec(memory_space=pltpu.VMEM)
    turned = jax.ShapeDtypeStruct((TEAM * TILES, DIM, WIDE), BF16)
    return pl.pallas_call(
        stats_kernel,
        out_shape=(jax.ShapeDtypeStruct((TEAM, 8, WIDE), F32), turned, turned),
        in_specs=[smem] + [vmem] * 12,
        out_specs=(vmem, vmem, vmem),
        scratch_shapes=[
            pltpu.VMEM((TEAM, ROWS, 2 * DIM), BF16),
            pltpu.VMEM((TEAM * TILES, DIM, WIDE), BF16),
            pltpu.VMEM((TEAM * TILES, 8, WIDE), F32),
            pltpu.VMEM((TEAM, ROWS, DIM), BF16),
        ],
        compiler_params=pltpu.CompilerParams(vmem_limit_bytes=VMEM_LIMIT),
    )(scal, *q_slots, *s_slots, *kvs)


def split3(value):
    high = value.astype(BF16)
    rest = value - high.astype(F32)
    mid = rest.astype(BF16)
    low = (rest - mid.astype(F32)).astype(BF16)
    return high, mid, low


def grads_kernel(scal, *refs):
    stat_refs, q_refs, s_refs, kv_refs = refs[0:4], refs[4:8], refs[8:12], refs[12:16]
    qt_ref, st_ref = refs[16:18]
    dq_own_ref, dq_far_ref, dq_core_ref, kv_own_ref = refs[18:22]
    kv_send_refs = refs[22:25]
    kx_ref, vx_ref, kt_ref, qn_ref, sn_ref, qa_ref, sa_ref, dq_ref, dk_ref, dv_ref = refs[25:35]
    fill_keys(scal, kv_refs, kx_ref, vx_ref, kt_ref)
    qa_ref[...] = jnp.zeros_like(qa_ref)
    sa_ref[...] = jnp.zeros_like(sa_ref)
    dq_ref[...] = jnp.zeros_like(dq_ref)
    dk_ref[...] = jnp.zeros_like(dk_ref)
    dv_ref[...] = jnp.zeros_like(dv_ref)
    row16 = lax.broadcasted_iota(jnp.int32, (16, WIDE), 0)

    def rows_of(values):
        out = jnp.zeros((16, WIDE), F32)
        for index, value in enumerate(values):
            out = jnp.where(row16 == index, value.astype(F32), out)
        return out.astype(BF16)

    for slot in range(TEAM):
        for at in range(TILES):
            n = slot * TILES + at
            for h in range(HEADS):
                cut = (slice(at * TILE, (at + 1) * TILE), slice(h * DIM, (h + 1) * DIM))
                qn_ref[n, h * TILE : (h + 1) * TILE] = q_refs[slot][cut]
                sn_ref[n, h * TILE : (h + 1) * TILE] = s_refs[slot][cut]
            sums = [stat_refs[e][slot ^ e, at : at + 1] for e in range(TEAM)]
            deltas = [stat_refs[e][slot ^ e, 3 + at : 4 + at] for e in range(TEAM)]
            top = functools.reduce(jnp.maximum, sums)
            weights = [jnp.exp2((one - top) * SCALE) for one in sums]
            total = sum(weights)
            whole = top + jnp.log2(total) * (1.0 / SCALE)
            delta = sum(w * x for w, x in zip(weights, deltas)) / total
            qa_ref[n, :16] = rows_of(split3(-whole) + (row_flags(scal, slot, at),))
            sa_ref[n, :16] = rows_of(split3(-delta))

    def job(slot, at, d, j0, keys, kind):
        n = slot * TILES + at
        part = slice(j0, j0 + keys)
        logits = dot(kx_ref[d, part], jnp.concatenate([qt_ref[n], qa_ref[n]], axis=0))
        p = jnp.exp2(logits * SCALE)
        if kind is not None:
            p = jnp.where(mask_of(kind, keys), p, 0.0)
        dp = dot(vx_ref[d, part], jnp.concatenate([st_ref[n], sa_ref[n]], axis=0))
        ds = (p * dp).astype(BF16)
        dv_ref[d, part] += dot(p.astype(BF16), sn_ref[n])
        dk_ref[d, part] += dot(ds, qn_ref[n])
        dq_ref[n] += dot(kt_ref[d, :, part], ds)

    def step(index, carry):
        base = HEAD_SCALARS + 3 * index
        job(scal[base], scal[base + 1], scal[base + 2], 0, ROWS, None)
        return carry

    lax.fori_loop(0, len(FULL), step, 0)
    for one in masked_jobs(scal):
        job(*one)

    outs = {0: dq_own_ref, 2: dq_far_ref, 1: dq_core_ref.at[0], 3: dq_core_ref.at[1]}
    for slot in range(TEAM):
        for at in range(TILES):
            for h in range(HEADS):
                block = dq_ref[slot * TILES + at, :, h * TILE : (h + 1) * TILE] * FACTOR
                outs[slot][at * TILE : (at + 1) * TILE, h * DIM : (h + 1) * DIM] = block.T.astype(
                    outs[slot].dtype
                )
    kv_own_ref[:ROWS] = dk_ref[0] * FACTOR
    kv_own_ref[ROWS:] = dv_ref[0]
    for d in range(1, TEAM):
        kv_send_refs[d - 1][:ROWS] = (dk_ref[d] * FACTOR).astype(BF16)
        kv_send_refs[d - 1][ROWS:] = dv_ref[d].astype(BF16)


def grads_of(scal, stats, q_slots, s_slots, kvs, turned_q, turned_s):
    smem = pl.BlockSpec(memory_space=pltpu.SMEM)
    vmem = pl.BlockSpec(memory_space=pltpu.VMEM)
    shape = jax.ShapeDtypeStruct
    blocks = TEAM * TILES
    return pl.pallas_call(
        grads_kernel,
        out_shape=(
            shape((ROWS, HEADS * DIM), F32),
            shape((ROWS, HEADS * DIM), F32),
            shape((2, ROWS, HEADS * DIM), BF16),
            shape((2 * ROWS, DIM), F32),
        )
        + (shape((2 * ROWS, DIM), BF16),) * 3,
        in_specs=[smem] + [vmem] * 18,
        out_specs=(vmem,) * 7,
        scratch_shapes=[
            pltpu.VMEM((TEAM, ROWS, 2 * DIM), BF16),
            pltpu.VMEM((TEAM, ROWS, 2 * DIM), BF16),
            pltpu.VMEM((TEAM, DIM, ROWS), BF16),
            pltpu.VMEM((blocks, WIDE, DIM), BF16),
            pltpu.VMEM((blocks, WIDE, DIM), BF16),
            pltpu.VMEM((blocks, DIM, WIDE), BF16),
            pltpu.VMEM((blocks, DIM, WIDE), BF16),
            pltpu.VMEM((blocks, DIM, WIDE), F32),
            pltpu.VMEM((TEAM, ROWS, DIM), F32),
            pltpu.VMEM((TEAM, ROWS, DIM), F32),
        ],
        compiler_params=pltpu.CompilerParams(vmem_limit_bytes=VMEM_LIMIT),
    )(scal, *stats, *q_slots, *s_slots, *kvs, turned_q, turned_s)


def team_slots(value):
    core = permute(value, lambda s: s ^ 1)
    far = permute(value, lambda s: s ^ 2)
    both = permute(far, lambda s: s ^ 1)
    return [value, core, far, both]


def per_device(queries, key_rows, value_rows, positions, latent_ids, latent_acts, latent_dirs):
    kv = jnp.concatenate([key_rows, value_rows], axis=0)
    kvs = [kv] + [permute(kv, lambda s, d=d: s + TEAM * d) for d in range(1, TEAM)]
    q_slots = team_slots(queries)
    s_slots = team_slots(seeds_of(latent_ids, latent_acts, latent_dirs))
    scal = scalars_of(positions)
    stat, turned_q, turned_s = stats_of(scal, q_slots, s_slots, kvs)
    stats = [stat] + [permute(stat, lambda s, e=e: s ^ e) for e in range(1, TEAM)]
    dq_own, dq_far, dq_core, kv_own, *kv_send = grads_of(
        scal, stats, q_slots, s_slots, kvs, turned_q, turned_s
    )
    kv_back = [
        permute(send, lambda s, d=d: s - TEAM * d) for d, send in enumerate(kv_send, 1)
    ]
    dq_near = permute(dq_core, lambda s: s ^ 1).astype(F32)
    dq_back = permute((dq_far + dq_near[1]).astype(BF16), lambda s: s ^ 2)
    grad_q = (dq_own + dq_near[0] + dq_back.astype(F32)).astype(BF16)
    grad_kv = kv_own + sum(part.astype(F32) for part in kv_back)
    grad_k = grad_kv[:ROWS].astype(BF16)
    grad_v = grad_kv[ROWS:].astype(BF16)
    return grad_q, grad_k, grad_v


def solution(mesh):
    in_specs = (
        P(("mp", "ctx"), None),
        P(("mp", "ctx"), None),
        P(("mp", "ctx"), None),
        P("ctx"),
        P(("mp", "ctx"), None),
        P(("mp", "ctx"), None),
        P("mp", None),
    )
    out_specs = (P(("mp", "ctx"), None), P(("mp", "ctx"), None), P(("mp", "ctx"), None))
    return jax.shard_map(
        per_device, mesh=mesh, in_specs=in_specs, out_specs=out_specs, check_vma=False
    )
```

time: 365 us -> 139 us (0.38)
  waiting for transfers between devices: 167 us -> 43.9 us
  matrix products: 74.2 us -> 0 us
  starting transfers between devices: 77.4 us -> 26.4 us
  Pallas kernels: 0 us -> 51 us
  other arithmetic: 22.4 us -> 5.21 us
  local copies, waits for them, and re-layouts: 22.4 us -> 8.51 us
    ppermute x22 -> x17, waiting for transfers between devices: 167 us -> 43.9 us  [permute(): lax.ppermute(value, 'ctx', [(s, target(s) % count) for s in range(count)])]
    dot_general x21 -> x0, matrix products: 74.2 us -> none  [the longest x4 27.5 us: per_head(): jnp.dot(probs_b.T, seed_one, preferred_element_type=jnp.float32)]
    ppermute x22 -> x17, starting transfers between devices: 77.4 us -> 26.4 us  [permute(): lax.ppermute(value, 'ctx', [(s, target(s) % count) for s in range(count)])]
    pallas_call x0 -> x3, Pallas kernels: none -> 51 us  [the longest x1 28.1 us: grads_of(): pl.pallas_call(grads_kernel, out_shape=(shape((ROWS, HEADS * DIM), F32),...]
    while x32 -> x0, local copies, waits for them, and re-layouts: 11.5 us -> none
    convert_element_type x4, other arithmetic: 11 us -> 1.34 us  [the longest x1 0.96 us: per_device(): grad_q = (dq_own + dq_near[0] + dq_back.astype(F32)).astype(BF16)]
    reduce_sum x5 -> x0, other arithmetic: 7.77 us -> none  [the longest x4 4.36 us: per_head(): totals = jnp.sum(expos, axis=-1, keepdims=True)]
    unnamed x28 -> x47, local copies, waits for them, and re-layouts: 7.57 us -> 3.36 us
  transfers between devices with their start and end apart: 22 -> 17, of which waited for: 22 -> 7; matrix products, arithmetic and copies ran while one was open for 3% -> 7% of each run, Pallas kernels for 0% -> 0%
where the time goes in v1:
time: 139 us; the launch traced here: 138 us
  Pallas kernels  51 us (37%)
  waiting for transfers between devices  43.9 us (32%)
  starting transfers between devices  26.4 us (19%)
  local copies, waits for them, and re-layouts  8.51 us (6%)
  other arithmetic  5.21 us (4%)
  between operations  2.85 us (2%)
    ppermute x17, waiting for transfers between devices, permute(): lax.ppermute(value, 'ctx', [(s, target(s) % count) for s in range(count)])  43.9 us
    pallas_call x1, Pallas kernels, grads_of(): pl.pallas_call(grads_kernel, out_shape=(shape((ROWS, HEADS * DIM), F32),...  28.1 us
    ppermute x17, starting transfers between devices, permute(): lax.ppermute(value, 'ctx', [(s, target(s) % count) for s in range(count)])  26.4 us
    pallas_call x1, Pallas kernels, stats_of(): pl.pallas_call(stats_kernel, out_shape=(jax.ShapeDtypeStruct((TEAM, 8, WI...  18.7 us
    pallas_call x1, Pallas kernels, seeds_of(): pl.pallas_call(seed_kernel, out_shape=jax.ShapeDtypeStruct((latent_ids.sh...  4.17 us
    another operation x2, other arithmetic, scalars_of(): jnp.stack([slots[jobs[:, 0]], jobs[:, 1], jobs[:, 2] + wraps[jobs[:, 0]]]...  3.77 us
    unnamed x47, local copies, waits for them, and re-layouts  3.36 us
  transfers between devices with their start and end apart: 17, of which 7 were waited for; matrix products, arithmetic and copies ran while one was open for 7% of the time, Pallas kernels for 0%

profile of v1, /device:TPU:2, one launch (start us, length us, event | category | flops | bytes accessed | tf_op | source)
XLA Modules:
  0.0 137.8 jit_solution(18027770071067724305)
XLA Ops:
  0.6 0.0 copy-start.20
  0.6 0.0 copy-start.21
  0.7 0.0 copy-start.22
  0.7 0.0 copy-start.19
  0.7 0.0 copy-start
  0.7 4.2 %shard_map.103.refs_4_.refs_8_ = bf16[384,512]{1,0:T(8,128)(2,1)} custom-call(s32[8,384]{1,0:T(8,128)} %bitcast.26, f32[8,384]{1,0:T(8,128)} %bitcast.27, f32[512,512]{1,0:T(8,128)} %dirs_ref.1), custom_call_target="tpu_custom_call" | custom-call | tf_op jit(solution)/shard_map/pallas_call | solution.py:54
  4.9 2.1 %collective-permute-start.4 = (bf16[384,512]{1,0:T(8,128)(2,1)}, bf16[384,512]{1,0:T(8,128)(2,1)S(1)}, u32[]{:S(2)}, u32[]{:S(2)}) collective-permute-start(bf16[384,512]{1,0:T(8,128)(2,1)} %shard_map.103.refs_4_.refs_8_), channel_id=1, source_target_pairs={{0,4},{2,6},{4,0},{6,2},{8,12},{10,14},{12,8},{14,10},{16,20},{18,... | collective-permute-start | bytes 1179656 | tf_op jit(solution)/shard_map/ppermute | solution.py:30
  7.0 1.4 %collective-permute-start.1 = (bf16[384,512]{1,0:T(8,128)(2,1)}, bf16[384,512]{1,0:T(8,128)(2,1)S(1)}, u32[]{:S(2)}, u32[]{:S(2)}) collective-permute-start(bf16[384,512]{1,0:T(8,128)(2,1)} %refs_4_.1), channel_id=1, source_target_pairs={{0,4},{2,6},{4,0},{6,2},{8,12},{10,14},{12,8},{14,10},{16,20},{18,... | collective-permute-start | bytes 1179656 | tf_op jit(solution)/shard_map/ppermute | solution.py:30
  8.4 0.9 constant_dynamic-update-slice_fusion.1
  9.3 4.7 %collective-permute-start.8 = (bf16[768,128]{1,0:T(8,128)(2,1)S(1)}, bf16[768,128]{1,0:T(8,128)(2,1)S(1)}, u32[]{:S(2)}, u32[]{:S(2)}) collective-permute-start(bf16[768,128]{1,0:T(8,128)(2,1)S(1)} %constant_dynamic-update-slice_fusion.refs_8_.refs_12_), channel_id=1, source_target_pairs={{0,24},{2,26},{4,28},{6,30},{8,32},{10,34},{12,36},{14,38},{16,40}... | collective-permute-start | bytes 589832 | tf_op jit(solution)/shard_map/ppermute | solution.py:30
  14.0 3.6 %collective-permute-start.7 = (bf16[768,128]{1,0:T(8,128)(2,1)S(1)}, bf16[768,128]{1,0:T(8,128)(2,1)S(1)}, u32[]{:S(2)}, u32[]{:S(2)}) collective-permute-start(bf16[768,128]{1,0:T(8,128)(2,1)S(1)} %constant_dynamic-update-slice_fusion.refs_8_.refs_12_), channel_id=1, source_target_pairs={{0,16},{2,18},{4,20},{6,22},{8,24},{10,26},{12,28},{14,30},{16,32}... | collective-permute-start | bytes 589832 | tf_op jit(solution)/shard_map/ppermute | solution.py:30
  17.6 0.0 collective-permute-start.3
  17.6 14.9 %collective-permute-done.8.refs_11_.refs_15_ = bf16[768,128]{1,0:T(8,128)(2,1)S(1)} collective-permute-done((bf16[768,128]{1,0:T(8,128)(2,1)S(1)}, bf16[768,128]{1,0:T(8,128)(2,1)S(1)}, u32[]{:S(2)}, u32[]{:S(2)}) %collective-permute-start.8) | collective-permute-done | bytes 196640 | tf_op jit(solution)/shard_map/ppermute | solution.py:30
  32.6 0.0 copy-done
  32.6 0.0 collective-permute-start
  32.6 0.0 collective-permute-done.4.refs_6_.refs_10_
  32.6 0.5 collective-permute-start.5
  33.1 0.0 collective-permute-done.1.refs_2_.refs_6_
  33.1 0.1 collective-permute-start.2
  33.2 0.6 fusion.7
  33.8 5.1 %collective-permute-done.7.refs_10_.refs_14_ = bf16[768,128]{1,0:T(8,128)(2,1)S(1)} collective-permute-done((bf16[768,128]{1,0:T(8,128)(2,1)S(1)}, bf16[768,128]{1,0:T(8,128)(2,1)S(1)}, u32[]{:S(2)}, u32[]{:S(2)}) %collective-permute-start.7) | collective-permute-done | bytes 196640 | tf_op jit(solution)/shard_map/ppermute | solution.py:30
  38.9 1.6 %collective-permute-start.6 = (bf16[768,128]{1,0:T(8,128)(2,1)S(1)}, bf16[768,128]{1,0:T(8,128)(2,1)S(1)}, u32[]{:S(2)}, u32[]{:S(2)}) collective-permute-start(bf16[768,128]{1,0:T(8,128)(2,1)S(1)} %constant_dynamic-update-slice_fusion.refs_8_.refs_12_), channel_id=1, source_target_pairs={{0,8},{2,10},{4,12},{6,14},{8,16},{10,18},{12,20},{14,22},{16,24},... | collective-permute-start | bytes 589832 | tf_op jit(solution)/shard_map/ppermute | solution.py:30
  40.5 3.2 %select_bitcast_fusion = (s32[29,1]{0,1:T(1,128)S(1)}, s32[29,1]{0,1:T(1,128)S(1)}) fusion(pred[29]{0:T(512)(128)(4,1)S(1)} %copy-done.22, pred[29]{0:T(512)(128)(4,1)S(1)} %copy-done.21, pred[29]{0:T(512)(128)(4,1)S(1)} %copy-done.20, s32[]{:T(128)} %add_shard_map.3, s32[]{:T(128)} %sub.8, s32[29]{0:T(128)} %constant.58, s32[]{:T(128)} %bitcast.6, ...), kind=kLoop, calls=%fused_computation.14 | loop fusion | flops 203 | bytes 459 | tf_op jit(solution)/shard_map/stack | solution.py:87
  43.7 1.2 slice.27
  46.8 0.6 pad_add_fusion
  47.4 0.8 copy.12
  48.2 0.6 reshape.17
  48.8 1.2 concatenate.6.scal
  50.0 0.0 collective-permute-done.6.refs_9_.refs_13_
  50.1 0.0 collective-permute-done.3.refs_5_.refs_9_
  50.1 0.0 collective-permute-done.refs_1_.refs_5_
  50.1 0.0 copy-start.4
  50.1 0.0 collective-permute-done.5.refs_7_.refs_11_
  50.1 0.0 collective-permute-done.2.refs_3_.refs_7_
  50.2 0.6 copy-done.12
  50.7 0.1 copy-done.3
  50.9 0.1 copy-done.4
  51.0 0.2 copy-done.5
  51.2 0.7 copy-done.6
  51.9 18.7 %shard_map.104 = (f32[4,8,512]{2,1,0:T(8,128)}, bf16[12,128,512]{2,1,0:T(8,128)(2,1)}, bf16[12,128,512]{2,1,0:T(8,128)(2,1)}) custom-call(s32[95]{0:T(128)} %concatenate.6.scal, bf16[384,512]{1,0:T(8,128)(2,1)} %refs_4_.1, bf16[384,512]{1,0:T(8,128)(2,1)} %copy-done.4, bf16[384,512]{1,0:T(8,128)(2,1)} %copy-done.2, bf16[384,512]{1,0:T(8,128)(2,1)} %copy-done.6, ...), custom_call_target="tpu_custom_call" | custom-call | tf_op jit(solution)/shard_map/pallas_call | solution.py:203
  70.6 0.4 collective-permute-start.11
  71.0 2.0 %collective-permute-start.10 = (f32[4,8,512]{2,1,0:T(8,128)}, f32[4,8,512]{2,1,0:T(8,128)S(1)}, u32[]{:S(2)}, u32[]{:S(2)}) collective-permute-start(f32[4,8,512]{2,1,0:T(8,128)} %get-tuple-element.13.refs_0_), channel_id=1, source_target_pairs={{0,4},{2,6},{4,0},{6,2},{8,12},{10,14},{12,8},{14,10},{16,20},{18,... | collective-permute-start | bytes 196616 | tf_op jit(solution)/shard_map/ppermute | solution.py:30
  73.0 1.0 collective-permute-start.9
  74.0 2.0 %collective-permute-done.11.refs_3_ = f32[4,8,512]{2,1,0:T(8,128)S(1)} collective-permute-done((f32[4,8,512]{2,1,0:T(8,128)}, f32[4,8,512]{2,1,0:T(8,128)S(1)}, u32[]{:S(2)}, u32[]{:S(2)}) %collective-permute-start.11) | collective-permute-done | bytes 65568 | tf_op jit(solution)/shard_map/ppermute | solution.py:30
  76.0 1.0 collective-permute-done.10.refs_2_
  77.0 0.0 collective-permute-done.9.refs_1_
  77.0 0.6 copy-done.16
  77.6 0.0 copy-done.17
  77.7 28.1 %shard_map.105 = (f32[384,512]{1,0:T(8,128)}, f32[384,512]{1,0:T(8,128)}, bf16[2,384,512]{2,1,0:T(8,128)(2,1)}, f32[768,128]{1,0:T(8,128)}, bf16[768,128]{1,0:T(...) custom-call(s32[95]{0:T(128)} %concatenate.6.scal, f32[4,8,512]{2,1,0:T(8,128)} %get-tuple-element.13.refs_0_, ...), custom_call_target="tpu_custom_call" | custom-call | tf_op jit(solution)/shard_map/pallas_call | solution.py:305
  105.8 0.8 collective-permute-start.12
  106.5 3.8 %collective-permute-start.14 = (bf16[768,128]{1,0:T(8,128)(2,1)}, bf16[768,128]{1,0:T(8,128)(2,1)S(1)}, u32[]{:S(2)}, u32[]{:S(2)}) collective-permute-start(bf16[768,128]{1,0:T(8,128)(2,1)} %get-tuple-element.20), channel_id=1, source_target_pairs={{0,248},{2,250},{4,252},{6,254},{8,0},{10,2},{12,4},{14,6},{16,8},... | collective-permute-start | bytes 589832 | tf_op jit(solution)/shard_map/ppermute | solution.py:30
  110.3 1.1 collective-permute-start.15
  111.4 1.4 %collective-permute-start.16 = (bf16[768,128]{1,0:T(8,128)(2,1)}, bf16[768,128]{1,0:T(8,128)(2,1)S(1)}, u32[]{:S(2)}, u32[]{:S(2)}) collective-permute-start(bf16[768,128]{1,0:T(8,128)(2,1)} %get-tuple-element.22), channel_id=1, source_target_pairs={{0,232},{2,234},{4,236},{6,238},{8,240},{10,242},{12,244},{14,246}... | collective-permute-start | bytes 589832 | tf_op jit(solution)/shard_map/ppermute | solution.py:30
  112.9 0.0 collective-permute-done.12
  112.9 0.2 convert_element_type.27
  113.1 0.2 fusion.1
  113.3 2.0 %collective-permute-start.13 = (bf16[384,512]{1,0:T(8,128)(2,1)S(1)}, bf16[384,512]{1,0:T(8,128)(2,1)S(1)}, u32[]{:S(2)}, u32[]{:S(2)}) collective-permute-start(bf16[384,512]{1,0:T(8,128)(2,1)S(1)} %fusion.1), channel_id=1, source_target_pairs={{0,4},{2,6},{4,0},{6,2},{8,12},{10,14},{12,8},{14,10},{16,20},{18,... | collective-permute-start | bytes 1179656 | tf_op jit(solution)/shard_map/ppermute | solution.py:30
  115.3 4.2 %collective-permute-done.14 = bf16[768,128]{1,0:T(8,128)(2,1)S(1)} collective-permute-done((bf16[768,128]{1,0:T(8,128)(2,1)}, bf16[768,128]{1,0:T(8,128)(2,1)S(1)}, u32[]{:S(2)}, u32[]{:S(2)}) %collective-permute-start.14) | collective-permute-done | bytes 196640 | tf_op jit(solution)/shard_map/ppermute | solution.py:30
  119.5 11.0 %collective-permute-done.15 = bf16[768,128]{1,0:T(8,128)(2,1)S(1)} collective-permute-done((bf16[768,128]{1,0:T(8,128)(2,1)}, bf16[768,128]{1,0:T(8,128)(2,1)S(1)}, u32[]{:S(2)}, u32[]{:S(2)}) %collective-permute-start.15) | collective-permute-done | bytes 196640 | tf_op jit(solution)/shard_map/ppermute | solution.py:30
  130.4 5.6 %collective-permute-done.16 = bf16[768,128]{1,0:T(8,128)(2,1)S(1)} collective-permute-done((bf16[768,128]{1,0:T(8,128)(2,1)}, bf16[768,128]{1,0:T(8,128)(2,1)S(1)}, u32[]{:S(2)}, u32[]{:S(2)}) %collective-permute-start.16) | collective-permute-done | bytes 196640 | tf_op jit(solution)/shard_map/ppermute | solution.py:30
  136.1 0.1 add_convert_fusion
  136.2 0.7 fusion.6
  136.9 0.0 collective-permute-done.13
  136.9 1.0 fusion.4
  (34 shorter events, 0.1 us)
Async XLA Ops:
  0.6 39.9 %copy-start.20 = (pred[29]{0:T(512)(128)(4,1)S(1)}, pred[29]{0:T(512)(128)(4,1)}, u32[]{:S(2)}) copy-start(pred[29]{0:T(512)(128)(4,1)} %constant.71) | copy-start | bytes 91
  0.6 39.9 %copy-start.21 = (pred[29]{0:T(512)(128)(4,1)S(1)}, pred[29]{0:T(512)(128)(4,1)}, u32[]{:S(2)}) copy-start(pred[29]{0:T(512)(128)(4,1)} %constant.69) | copy-start | bytes 91
  0.7 39.9 %copy-start.22 = (pred[29]{0:T(512)(128)(4,1)S(1)}, pred[29]{0:T(512)(128)(4,1)}, u32[]{:S(2)}) copy-start(pred[29]{0:T(512)(128)(4,1)} %constant.68) | copy-start | bytes 91
  0.7 46.2 %copy-start.19 = (s32[29,1]{0,1:T(1,128)S(1)}, s32[29,1]{0,1:T(1,128)}, u32[]{:S(2)}) copy-start(s32[29,1]{0,1:T(1,128)} %constant.56) | copy-start | bytes 352
  0.7 31.9 %copy-start = (bf16[384,512]{1,0:T(8,128)(2,1)S(1)}, bf16[384,512]{1,0:T(8,128)(2,1)}, u32[]{:S(2)}) copy-start(bf16[384,512]{1,0:T(8,128)(2,1)} %refs_4_.1) | copy-start | bytes 1179652
  0.7 8.6 %copy-start.14 = (bf16[384,128]{1,0:T(8,128)(2,1)S(1)}, bf16[384,128]{1,0:T(8,128)(2,1)}, u32[]{:S(2)}) copy-start(bf16[384,128]{1,0:T(8,128)(2,1)} %param.10) | copy-start | bytes 294916
  4.9 27.7 %collective-permute-start.4 = (bf16[384,512]{1,0:T(8,128)(2,1)}, bf16[384,512]{1,0:T(8,128)(2,1)S(1)}, u32[]{:S(2)}, u32[]{:S(2)}) collective-permute-start(bf16[384,512]{1,0:T(8,128)(2,1)} %shard_map.103.refs_4_.refs_8_), channel_id=1, source_target_pairs={{0,4},{2,6},{4,0},{6,2},{8,12},{10,14},{12,8},{14,10},{16,20},{18,... | collective-permute-start | bytes 1179656 | tf_op jit(solution)/shard_map/ppermute | solution.py:30
  7.0 26.1 %collective-permute-start.1 = (bf16[384,512]{1,0:T(8,128)(2,1)}, bf16[384,512]{1,0:T(8,128)(2,1)S(1)}, u32[]{:S(2)}, u32[]{:S(2)}) collective-permute-start(bf16[384,512]{1,0:T(8,128)(2,1)} %refs_4_.1), channel_id=1, source_target_pairs={{0,4},{2,6},{4,0},{6,2},{8,12},{10,14},{12,8},{14,10},{16,20},{18,... | collective-permute-start | bytes 1179656 | tf_op jit(solution)/shard_map/ppermute | solution.py:30
  9.3 40.8 %copy-start.7 = (bf16[768,128]{1,0:T(8,128)(2,1)}, bf16[768,128]{1,0:T(8,128)(2,1)S(1)}, u32[]{:S(2)}) copy-start(bf16[768,128]{1,0:T(8,128)(2,1)S(1)} %constant_dynamic-update-slice_fusion.refs_8_.refs_12_) | copy-start | bytes 589828
  9.3 23.2 %collective-permute-start.8 = (bf16[768,128]{1,0:T(8,128)(2,1)S(1)}, bf16[768,128]{1,0:T(8,128)(2,1)S(1)}, u32[]{:S(2)}, u32[]{:S(2)}) collective-permute-start(bf16[768,128]{1,0:T(8,128)(2,1)S(1)} %constant_dynamic-update-slice_fusion.refs_8_.refs_12_), channel_id=1, source_target_pairs={{0,24},{2,26},{4,28},{6,30},{8,32},{10,34},{12,36},{14,38},{16,40}... | collective-permute-start | bytes 589832 | tf_op jit(solution)/shard_map/ppermute | solution.py:30
  14.0 24.9 %collective-permute-start.7 = (bf16[768,128]{1,0:T(8,128)(2,1)S(1)}, bf16[768,128]{1,0:T(8,128)(2,1)S(1)}, u32[]{:S(2)}, u32[]{:S(2)}) collective-permute-start(bf16[768,128]{1,0:T(8,128)(2,1)S(1)} %constant_dynamic-update-slice_fusion.refs_8_.refs_12_), channel_id=1, source_target_pairs={{0,16},{2,18},{4,20},{6,22},{8,24},{10,26},{12,28},{14,30},{16,32}... | collective-permute-start | bytes 589832 | tf_op jit(solution)/shard_map/ppermute | solution.py:30
  17.6 32.4 %collective-permute-start.3 = (bf16[384,512]{1,0:T(8,128)(2,1)}, bf16[384,512]{1,0:T(8,128)(2,1)S(1)}, u32[]{:S(2)}, u32[]{:S(2)}) collective-permute-start(bf16[384,512]{1,0:T(8,128)(2,1)} %shard_map.103.refs_4_.refs_8_), channel_id=1, source_target_pairs={{0,2},{2,0},{4,6},{6,4},{8,10},{10,8},{12,14},{14,12},{16,18},{18,... | collective-permute-start | bytes 1179656 | tf_op jit(solution)/shard_map/ppermute | solution.py:30
  17.6 15.6 %copy-start.18 = (s32[4]{0:T(128)}, s32[4]{0:T(128)S(1)}, u32[]{:S(2)}) copy-start(s32[4]{0:T(128)S(1)} %compare_convert_fusion) | copy-start | bytes 52
  32.6 17.6 %copy-start.10 = (bf16[768,128]{1,0:T(8,128)(2,1)}, bf16[768,128]{1,0:T(8,128)(2,1)S(1)}, u32[]{:S(2)}) copy-start(bf16[768,128]{1,0:T(8,128)(2,1)S(1)} %collective-permute-done.8.refs_11_.refs_15_) | copy-start | bytes 589828
  32.6 17.5 %collective-permute-start = (bf16[384,512]{1,0:T(8,128)(2,1)S(1)}, bf16[384,512]{1,0:T(8,128)(2,1)S(1)}, u32[]{:S(2)}, u32[]{:S(2)}) collective-permute-start(bf16[384,512]{1,0:T(8,128)(2,1)S(1)} %copy-done), channel_id=1, source_target_pairs={{0,2},{2,0},{4,6},{6,4},{8,10},{10,8},{12,14},{14,12},{16,18},{18,... | collective-permute-start | bytes 1179656 | tf_op jit(solution)/shard_map/ppermute | solution.py:30
  32.6 17.6 %copy-start.1 = (bf16[384,512]{1,0:T(8,128)(2,1)}, bf16[384,512]{1,0:T(8,128)(2,1)S(1)}, u32[]{:S(2)}) copy-start(bf16[384,512]{1,0:T(8,128)(2,1)S(1)} %collective-permute-done.4.refs_6_.refs_10_) | copy-start | bytes 1179652
  32.6 17.5 %collective-permute-start.5 = (bf16[384,512]{1,0:T(8,128)(2,1)S(1)}, bf16[384,512]{1,0:T(8,128)(2,1)S(1)}, u32[]{:S(2)}, u32[]{:S(2)}) collective-permute-start(bf16[384,512]{1,0:T(8,128)(2,1)S(1)} %collective-permute-done.4.refs_6_.refs_10_), channel_id=1, source_target_pairs={{0,2},{2,0},{4,6},{6,4},{8,10},{10,8},{12,14},{14,12},{16,18},{18,... | collective-permute-start | bytes 1179656 | tf_op jit(solution)/shard_map/ppermute | solution.py:30
  33.1 17.1 %copy-start.2 = (bf16[384,512]{1,0:T(8,128)(2,1)}, bf16[384,512]{1,0:T(8,128)(2,1)S(1)}, u32[]{:S(2)}) copy-start(bf16[384,512]{1,0:T(8,128)(2,1)S(1)} %collective-permute-done.1.refs_2_.refs_6_) | copy-start | bytes 1179652
  33.1 17.0 %collective-permute-start.2 = (bf16[384,512]{1,0:T(8,128)(2,1)S(1)}, bf16[384,512]{1,0:T(8,128)(2,1)S(1)}, u32[]{:S(2)}, u32[]{:S(2)}) collective-permute-start(bf16[384,512]{1,0:T(8,128)(2,1)S(1)} %collective-permute-done.1.refs_2_.refs_6_), channel_id=1, source_target_pairs={{0,2},{2,0},{4,6},{6,4},{8,10},{10,8},{12,14},{14,12},{16,18},{18,... | collective-permute-start | bytes 1179656 | tf_op jit(solution)/shard_map/ppermute | solution.py:30
  38.9 11.2 %copy-start.11 = (bf16[768,128]{1,0:T(8,128)(2,1)}, bf16[768,128]{1,0:T(8,128)(2,1)S(1)}, u32[]{:S(2)}) copy-start(bf16[768,128]{1,0:T(8,128)(2,1)S(1)} %collective-permute-done.7.refs_10_.refs_14_) | copy-start | bytes 589828
  38.9 11.1 %collective-permute-start.6 = (bf16[768,128]{1,0:T(8,128)(2,1)S(1)}, bf16[768,128]{1,0:T(8,128)(2,1)S(1)}, u32[]{:S(2)}, u32[]{:S(2)}) collective-permute-start(bf16[768,128]{1,0:T(8,128)(2,1)S(1)} %constant_dynamic-update-slice_fusion.refs_8_.refs_12_), channel_id=1, source_target_pairs={{0,8},{2,10},{4,12},{6,14},{8,16},{10,18},{12,20},{14,22},{16,24},... | collective-permute-start | bytes 589832 | tf_op jit(solution)/shard_map/ppermute | solution.py:30
  50.1 0.7 copy-start.12
  50.1 0.8 copy-start.3
  50.1 0.9 copy-start.4
  50.1 1.1 copy-start.5
  51.2 0.7 copy-start.6
  70.6 5.4 %collective-permute-start.11 = (f32[4,8,512]{2,1,0:T(8,128)}, f32[4,8,512]{2,1,0:T(8,128)S(1)}, u32[]{:S(2)}, u32[]{:S(2)}) collective-permute-start(f32[4,8,512]{2,1,0:T(8,128)} %get-tuple-element.13.refs_0_), channel_id=1, source_target_pairs={{0,6},{2,4},{4,2},{6,0},{8,14},{10,12},{12,10},{14,8},{16,22},{18,... | collective-permute-start | bytes 196616 | tf_op jit(solution)/shard_map/ppermute | solution.py:30
  71.0 6.0 %collective-permute-start.10 = (f32[4,8,512]{2,1,0:T(8,128)}, f32[4,8,512]{2,1,0:T(8,128)S(1)}, u32[]{:S(2)}, u32[]{:S(2)}) collective-permute-start(f32[4,8,512]{2,1,0:T(8,128)} %get-tuple-element.13.refs_0_), channel_id=1, source_target_pairs={{0,4},{2,6},{4,0},{6,2},{8,12},{10,14},{12,8},{14,10},{16,20},{18,... | collective-permute-start | bytes 196616 | tf_op jit(solution)/shard_map/ppermute | solution.py:30
  73.0 4.0 %collective-permute-start.9 = (f32[4,8,512]{2,1,0:T(8,128)}, f32[4,8,512]{2,1,0:T(8,128)S(1)}, u32[]{:S(2)}, u32[]{:S(2)}) collective-permute-start(f32[4,8,512]{2,1,0:T(8,128)} %get-tuple-element.13.refs_0_), channel_id=1, source_target_pairs={{0,2},{2,0},{4,6},{6,4},{8,10},{10,8},{12,14},{14,12},{16,18},{18,... | collective-permute-start | bytes 196616 | tf_op jit(solution)/shard_map/ppermute | solution.py:30
  76.0 1.0 copy-start.15
  77.0 0.6 copy-start.16
  77.0 0.6 copy-start.17
  105.7 7.3 %copy-start.9 = (f32[384,512]{1,0:T(8,128)S(1)}, f32[384,512]{1,0:T(8,128)}, u32[]{:S(2)}) copy-start(f32[384,512]{1,0:T(8,128)} %get-tuple-element.18) | copy-start | bytes 2359300
  105.8 7.1 %collective-permute-start.12 = (bf16[2,384,512]{2,1,0:T(8,128)(2,1)}, bf16[2,384,512]{2,1,0:T(8,128)(2,1)S(1)}, u32[]{:S(2)}, u32[]{:S(2)}) collective-permute-start(bf16[2,384,512]{2,1,0:T(8,128)(2,1)} %get-tuple-element.17), channel_id=1, source_target_pairs={{0,2},{2,0},{4,6},{6,4},{8,10},{10,8},{12,14},{14,12},{16,18},{18,... | collective-permute-start | bytes 2359304 | tf_op jit(solution)/shard_map/ppermute | solution.py:30
  106.5 12.9 %collective-permute-start.14 = (bf16[768,128]{1,0:T(8,128)(2,1)}, bf16[768,128]{1,0:T(8,128)(2,1)S(1)}, u32[]{:S(2)}, u32[]{:S(2)}) collective-permute-start(bf16[768,128]{1,0:T(8,128)(2,1)} %get-tuple-element.20), channel_id=1, source_target_pairs={{0,248},{2,250},{4,252},{6,254},{8,0},{10,2},{12,4},{14,6},{16,8},... | collective-permute-start | bytes 589832 | tf_op jit(solution)/shard_map/ppermute | solution.py:30
  110.3 20.1 %collective-permute-start.15 = (bf16[768,128]{1,0:T(8,128)(2,1)}, bf16[768,128]{1,0:T(8,128)(2,1)S(1)}, u32[]{:S(2)}, u32[]{:S(2)}) collective-permute-start(bf16[768,128]{1,0:T(8,128)(2,1)} %get-tuple-element.21), channel_id=1, source_target_pairs={{0,240},{2,242},{4,244},{6,246},{8,248},{10,250},{12,252},{14,254}... | collective-permute-start | bytes 589832 | tf_op jit(solution)/shard_map/ppermute | solution.py:30
  111.4 24.7 %collective-permute-start.16 = (bf16[768,128]{1,0:T(8,128)(2,1)}, bf16[768,128]{1,0:T(8,128)(2,1)S(1)}, u32[]{:S(2)}, u32[]{:S(2)}) collective-permute-start(bf16[768,128]{1,0:T(8,128)(2,1)} %get-tuple-element.22), channel_id=1, source_target_pairs={{0,232},{2,234},{4,236},{6,238},{8,240},{10,242},{12,244},{14,246}... | collective-permute-start | bytes 589832 | tf_op jit(solution)/shard_map/ppermute | solution.py:30
  113.1 23.0 %copy-start.13 = (f32[768,128]{1,0:T(8,128)S(1)}, f32[768,128]{1,0:T(8,128)}, u32[]{:S(2)}) copy-start(f32[768,128]{1,0:T(8,128)} %get-tuple-element.19) | copy-start | bytes 1179652
  113.1 23.8 %copy-start.8 = (f32[384,512]{1,0:T(8,128)S(1)}, f32[384,512]{1,0:T(8,128)}, u32[]{:S(2)}) copy-start(f32[384,512]{1,0:T(8,128)} %get-tuple-element.16) | copy-start | bytes 2359300
  113.3 23.6 %collective-permute-start.13 = (bf16[384,512]{1,0:T(8,128)(2,1)S(1)}, bf16[384,512]{1,0:T(8,128)(2,1)S(1)}, u32[]{:S(2)}, u32[]{:S(2)}) collective-permute-start(bf16[384,512]{1,0:T(8,128)(2,1)S(1)} %fusion.1), channel_id=1, source_target_pairs={{0,4},{2,6},{4,0},{6,2},{8,12},{10,14},{12,8},{14,10},{16,20},{18,... | collective-permute-start | bytes 1179656 | tf_op jit(solution)/shard_map/ppermute | solution.py:30
